TPU v7x, 32 devices: a whole 2x2x4 slice. The times are simulated.
32 devices in a mesh: frame: 16 (over z, x, core), head: 2 (over y).
Axes of the slice: x: 2, y: 2, z: 4, core: 2. Of those that a mesh axis runs over, the one named last changes fastest.
Arguments:
- queue: bfloat16 [2048, 5120], P('frame', 'head'), may hold values from -6 to 6
- noise_block: bfloat16 [64, 5120], P(None, 'head'), may hold values from -6 to 6
- w_query: bfloat16 [5120, 768], P('frame', 'head'), may hold values from -0.078125 to 0.078125
- w_key: bfloat16 [5120, 768], P('frame', 'head'), may hold values from -0.078125 to 0.078125
- w_value: bfloat16 [5120, 768], P('frame', 'head'), may hold values from -0.078125 to 0.078125
- w_output: bfloat16 [768, 5120], P('head', 'frame'), may hold values from -1.5 to 1.5
- mod_table: float32 [64, 3, 5120], replicated, may hold values from -4 to 4
- sigma_table: float32 [65], replicated, may hold values from 0 to 1
- timestep_index: int32 [32], P('frame'), may hold values from 0 to 63
- block_position: int32 [32], P('frame'), may hold values from 0 to 4095
Outputs:
- velocity: bfloat16 [2048, 5120], P('frame', 'head')
- queue_out: bfloat16 [2048, 5120], P('frame', 'head')
All inputs are finite; a program needn't handle non-finite values.
Results may differ from a plain program's by a relative error of at most 0.025.
Values may be sent and summed in bfloat16 or wider, within the bound.
A program may use at most 128 MiB of HBM per device.

v0:
```python
import math

import jax
import jax.numpy as jnp
from jax import lax
from jax.sharding import PartitionSpec as P

HEAD_SIZE = 128
REACH = 2


def with_halo(cells, sides, width):
    for axis, dim in sides:
        count = lax.axis_size(axis)
        ends = count - 1
        head = lax.slice_in_dim(cells, 0, width, axis=dim)
        tail = lax.slice_in_dim(cells, cells.shape[dim] - width, cells.shape[dim], axis=dim)
        cells = jnp.concatenate(
            [
                lax.ppermute(tail, axis, [(i, (i + 1) % count) for i in range(ends)]),
                cells,
                lax.ppermute(head, axis, [((i + 1) % count, i) for i in range(ends)]),
            ],
            axis=dim,
        )
    return cells


def passed_along(value, axis, steps):
    count = lax.axis_size(axis)
    leading, last = (max(0, -steps), min(count, count - steps))
    return lax.ppermute(value, axis, [(source, source + steps) for source in range(leading, last)])


def norm_heads(vectors):
    return vectors * lax.rsqrt(jnp.mean(vectors * vectors, axis=-1, keepdims=True) + 1e-06)


def rotate(vectors, positions):
    half_size = vectors.shape[-1] // 2
    freqs = 10000.0 ** (-jnp.arange(half_size, dtype=jnp.float32) / half_size)
    angles = positions.astype(jnp.float32)[:, None] * freqs[None, :]
    cosine = jnp.cos(angles)[:, None, None, :]
    sine = jnp.sin(angles)[:, None, None, :]
    first = vectors[..., :half_size]
    second = vectors[..., half_size:]
    return jnp.concatenate(
        [first * cosine - second * sine, first * sine + second * cosine], axis=-1
    )


def per_device(
    queue,
    noise_block,
    w_query,
    w_key,
    w_value,
    w_output,
    mod_table,
    sigma_table,
    timestep_index,
    block_position,
):
    row_count, feature_slab = queue.shape
    blocks_here = timestep_index.shape[0]
    block_rows = row_count // blocks_here
    frames = lax.axis_size("frame")
    frame_id = lax.axis_index("frame")
    head_id = lax.axis_index("head")
    query_full, key_full, value_full = (
        lax.all_gather(w_query, "frame", axis=0, tiled=True),
        lax.all_gather(w_key, "frame", axis=0, tiled=True),
        lax.all_gather(w_value, "frame", axis=0, tiled=True),
    )
    output_full = lax.all_gather(w_output, "frame", axis=1, tiled=True)
    levels = mod_table.shape[0]
    model_width = mod_table.shape[2]
    head_count = query_full.shape[1] // HEAD_SIZE
    inner_width = query_full.shape[1]
    one_hot = (timestep_index[:, None] == jnp.arange(levels, dtype=jnp.int32)[None, :]).astype(
        jnp.float32
    )
    modulation = jnp.dot(
        one_hot, mod_table.reshape(levels, 3 * model_width), precision=lax.Precision.HIGHEST
    ).reshape(blocks_here, 3, model_width)
    table_index = jnp.arange(sigma_table.shape[0], dtype=jnp.int32)[None, :]
    sigma_now = jnp.sum(
        jnp.where(timestep_index[:, None] == table_index, sigma_table[None, :], 0.0), axis=1
    )
    sigma_next = jnp.sum(
        jnp.where(timestep_index[:, None] + 1 == table_index, sigma_table[None, :], 0.0), axis=1
    )
    sigma_step = sigma_next - sigma_now
    gate_slab = lax.dynamic_slice_in_dim(
        modulation[:, 2, :], head_id * feature_slab, feature_slab, 1
    )
    shape4 = (blocks_here, block_rows, head_count, HEAD_SIZE)

    def attend(full_rows):
        wide_rows = full_rows.astype(jnp.float32).reshape(blocks_here, block_rows, model_width)
        row_mean = jnp.mean(wide_rows, axis=-1, keepdims=True)
        row_var = jnp.mean((wide_rows - row_mean) ** 2, axis=-1, keepdims=True)
        normed = (wide_rows - row_mean) * lax.rsqrt(row_var + 1e-06)
        modulated = (
            (normed * (1.0 + modulation[:, 1][:, None, :]) + modulation[:, 0][:, None, :])
            .astype(jnp.bfloat16)
            .reshape(row_count, model_width)
        )
        queries = rotate(
            norm_heads(
                jnp.dot(modulated, query_full, preferred_element_type=jnp.float32).reshape(shape4)
            ),
            block_position,
        ).astype(jnp.bfloat16)
        key_rows = rotate(
            norm_heads(
                jnp.dot(modulated, key_full, preferred_element_type=jnp.float32).reshape(shape4)
            ),
            block_position,
        ).astype(jnp.bfloat16)
        values = jnp.dot(modulated, value_full, preferred_element_type=jnp.float32).astype(
            jnp.bfloat16
        )
        key_value = jnp.stack([key_rows.reshape(row_count, inner_width), values], axis=1)
        beside_all = with_halo(key_value, (("frame", 0),), row_count)
        keys_all = beside_all[:, 0].reshape(3 * row_count, head_count, HEAD_SIZE)
        values_all = beside_all[:, 1].reshape(3 * row_count, head_count, HEAD_SIZE)
        query_block = frame_id * blocks_here + jnp.arange(row_count, dtype=jnp.int32) // block_rows
        key_block = (
            frame_id * blocks_here
            - blocks_here
            + jnp.arange(3 * row_count, dtype=jnp.int32) // block_rows
        )
        allowed = (
            (jnp.abs(query_block[:, None] - key_block[None, :]) <= REACH)
            & (key_block[None, :] >= 0)
            & (key_block[None, :] < frames * blocks_here)
        )
        scores = jnp.einsum(
            "qhd,khd->hqk",
            queries.reshape(row_count, head_count, HEAD_SIZE),
            keys_all,
            preferred_element_type=jnp.float32,
        ) / math.sqrt(HEAD_SIZE)
        raised = jnp.where(allowed[None, :, :], jnp.exp(scores), 0.0)
        weights = (raised / jnp.sum(raised, axis=-1, keepdims=True)).astype(jnp.bfloat16)
        attended = jnp.einsum(
            "hqk,khd->qhd", weights, values_all, preferred_element_type=jnp.float32
        )
        return attended.astype(jnp.bfloat16).reshape(row_count, inner_width)

    def gathered(queue_state):
        return lax.all_gather(queue_state, "head", axis=1, tiled=True)

    def reduced(attended):
        product = jnp.dot(attended, output_full, preferred_element_type=jnp.float32)
        return lax.psum_scatter(
            product.astype(jnp.bfloat16), "head", scatter_dimension=1, tiled=True
        ).astype(jnp.float32)

    def advance(base_rows, mixed_out):
        base_wide = base_rows.astype(jnp.float32).reshape(blocks_here, block_rows, feature_slab)
        layer_out = base_wide + gate_slab[:, None, :] * mixed_out.reshape(
            blocks_here, block_rows, feature_slab
        )
        following = base_wide + sigma_step[:, None, None] * layer_out
        return (
            layer_out.astype(jnp.bfloat16).reshape(row_count, feature_slab),
            following.astype(jnp.bfloat16).reshape(row_count, feature_slab),
        )

    attended_first = attend(gathered(queue))
    first_out, next_slab = advance(queue, reduced(attended_first))
    moved_in = passed_along(next_slab[:block_rows], "frame", -1)
    entering = jnp.where(frame_id == frames - 1, noise_block, moved_in)
    second_slab = jnp.concatenate([next_slab[block_rows:], entering], axis=0)
    attended_second = attend(gathered(second_slab))
    velocity, queue_out = advance(second_slab, reduced(attended_second))
    return (velocity, queue_out)


def solution(mesh):
    in_specs = (
        P("frame", "head"),
        P(None, "head"),
        P("frame", "head"),
        P("frame", "head"),
        P("frame", "head"),
        P("head", "frame"),
        P(),
        P(),
        P("frame"),
        P("frame"),
    )
    out_specs = (P("frame", "head"), P("frame", "head"))
    return jax.shard_map(
        per_device, mesh=mesh, in_specs=in_specs, out_specs=out_specs, check_vma=False
    )
```

profile of v0, /device:TPU:1, one launch (start us, length us, event | category | flops | bytes accessed | tf_op | source)
XLA Modules:
  0.0 360.5 jit_solution(16553343940943162823)
XLA Ops:
  7.2 0.7 all-gather.7.cloned.1.call-update
  7.9 0.7 all-gather.13.cloned.1.call-update
  8.7 0.7 all-gather.9.cloned.1.call-update
  9.4 0.5 all-gather.11.cloned.1.call-update
  10.0 0.5 all-gather.15.cloned.1.call-update
  10.6 0.7 convert_element_type.101
  11.3 0.1 multiply_cosine_fusion
  11.4 3.5 fusion
  14.9 21.0 %all-gather.7.cloned.1.call-done = bf16[128,5120]{1,0:T(8,128)(2,1)} async-done(((bf16[128,2560]{1,0:T(8,128)(2,1)}), bf16[128,5120]{1,0:T(8,128)(2,1)}) %all-gather.7.cloned.1.call-update) | async-done | bytes 1310736 | tf_op jit(solution)/shard_map/all_gather | solution.py:153
  35.9 1.7 convert_reduce_fusion.1
  37.6 1.8 fusion.8
  39.4 0.6 fusion.9
  40.0 47.4 %all-gather.13.cloned.1.call-done = bf16[5120,384]{1,0:T(8,128)(2,1)} async-done(((bf16[320,384]{1,0:T(8,128)(2,1)}), bf16[5120,384]{1,0:T(8,128)(2,1)}) %all-gather.13.cloned.1.call-update) | async-done | bytes 3932176 | tf_op jit(solution)/shard_map/all_gather | solution.py:71
  87.4 6.3 %copy.43 = bf16[384,5120]{1,0:T(8,128)(2,1)} copy(bf16[384,5120]{0,1:T(8,128)(2,1)} %bitcast.124) | data formatting | bytes 7864320 | tf_op jit(solution)/shard_map/dot_general | solution.py:111
  93.7 43.9 %all-gather.9.cloned.1.call-done = bf16[5120,384]{1,0:T(8,128)(2,1)} async-done(((bf16[320,384]{1,0:T(8,128)(2,1)}), bf16[5120,384]{1,0:T(8,128)(2,1)}) %all-gather.9.cloned.1.call-update) | async-done | bytes 3932176 | tf_op jit(solution)/shard_map/all_gather | solution.py:72
  137.6 6.2 %copy.40 = bf16[384,5120]{1,0:T(8,128)(2,1)} copy(bf16[384,5120]{0,1:T(8,128)(2,1)} %bitcast.125) | data formatting | bytes 7864320 | tf_op jit(solution)/shard_map/dot_general | solution.py:117
  143.9 3.7 %multiply_reduce_fusion.2 = (f32[2,64,3]{1,2,0:T(4,128)S(1)}, f32[2,64,3,128]{3,1,2,0:T(8,128)S(1)}) fusion(bf16[2,64,5120,1]{2,1,3,0:T(8,128)(2,1)S(1)} %bitcast.120, bf16[3,128,5120,1]{2,1,0,3:T(8,128)(2,1)} %bitcast.116), kind=kOutput, calls=%fused_computation.63 | convolution fusion | flops 503414400 | bytes 5441024 | tf_op jit(solution)/shard_map/dot_general | solution.py:111
  147.6 1.4 multiply_reduce_fusion.3
  149.0 0.2 broadcast_multiply_fusion.2
  149.2 0.2 subtract_convert_fusion.2
  149.4 0.1 pad_maximum_fusion.5
  149.7 38.0 %all-gather.11.cloned.1.call-done = bf16[5120,384]{1,0:T(8,128)(2,1)} async-done(((bf16[320,384]{1,0:T(8,128)(2,1)}), bf16[5120,384]{1,0:T(8,128)(2,1)}) %all-gather.11.cloned.1.call-update) | async-done | bytes 3932176 | tf_op jit(solution)/shard_map/all_gather | solution.py:73
  187.7 3.0 fusion.19
  190.7 2.2 collective-permute-start.1
  192.9 3.4 collective-permute-start
  196.3 0.1 fusion.24
  196.4 1.2 collective-permute-done.1
  197.7 4.3 %collective-permute-done = bf16[128,2,384]{2,0,1:T(8,128)(2,1)S(1)} collective-permute-done((bf16[128,2,384]{2,0,1:T(8,128)(2,1)S(1)}, bf16[128,2,384]{2,0,1:T(8,128)(2,1)S(1)}, u32[]{:S(2)}, u32[]{:S(2)}) %collective-permute-start) | collective-permute-done | bytes 196640 | tf_op jit(solution)/shard_map/ppermute | solution.py:20
  202.1 0.2 copy.48
  202.3 0.2 copy.42
  202.5 0.3 fusion.16
  202.8 0.4 convolution_convert_fusion.4
  203.2 34.9 %all-gather.15.cloned.1.call-done = bf16[384,5120]{0,1:T(8,128)(2,1)} async-done(((bf16[384,320]{0,1:T(8,128)(2,1)}), bf16[384,5120]{0,1:T(8,128)(2,1)}) %all-gather.15.cloned.1.call-update) | async-done | bytes 3932176 | tf_op jit(solution)/shard_map/all_gather | solution.py:75
  238.1 4.6 %convolution_convert_fusion.1 = bf16[128,5120]{1,0:T(8,128)(2,1)} fusion(bf16[128,384]{0,1:T(8,128)(2,1)S(1)} %bitcast.136, bf16[384,5120]{0,1:T(8,128)(2,1)} %all-gather.15.cloned.1.call-done), kind=kOutput, calls=%fused_computation.1 | convolution fusion | flops 503971840 | bytes 5341184 | tf_op jit(solution)/shard_map/dot_general | solution.py:156
  242.8 0.2 fusion.39
  243.1 21.7 %reduce-scatter.3.cloned.1.call-done = bf16[128,2560]{1,0:T(8,128)(2,1)} async-done(((bf16[128,5120]{1,0:T(8,128)(2,1)}), bf16[128,2560]{1,0:T(8,128)(2,1)}) %reduce-scatter.3.cloned.1.call-update) | async-done | bytes 655376 | tf_op jit(solution)/shard_map/reduce_scatter | solution.py:157
  264.8 1.4 fusion.13
  266.2 2.6 collective-permute-start.2
  268.8 5.8 %collective-permute-done.2 = bf16[64,2560]{1,0:T(8,128)(2,1)S(1)} collective-permute-done((bf16[64,2560]{1,0:T(8,128)(2,1)S(1)}, bf16[64,2560]{1,0:T(8,128)(2,1)S(1)}, u32[]{:S(2)}, u32[]{:S(2)}) %collective-permute-start.2) | collective-permute-done | bytes 327712 | tf_op jit(solution)/shard_map/ppermute | solution.py:32
  274.7 0.9 pad_maximum_fusion
  275.6 0.2 reduce-scatter.5.cloned.1.call-start
  275.8 23.6 %all-gather.17.cloned.1.call-done = bf16[128,5120]{1,0:T(8,128)(2,1)} async-done(((bf16[128,2560]{1,0:T(8,128)(2,1)}), bf16[128,5120]{1,0:T(8,128)(2,1)}) %all-gather.17.cloned.1.call-update) | async-done | bytes 1310736 | tf_op jit(solution)/shard_map/all_gather | solution.py:153
  299.4 1.7 convert_reduce_fusion
  301.2 1.8 fusion.7
  303.0 1.9 fusion.10
  304.9 1.4 multiply_reduce_fusion.1
  306.3 0.7 copy-done
  307.0 1.4 multiply_reduce_fusion
  308.5 0.1 broadcast_multiply_fusion
  308.6 0.1 broadcast_multiply_fusion.1
  308.7 0.2 subtract_convert_fusion
  308.9 0.1 pad_maximum_fusion.6
  309.2 3.0 fusion.20
  312.2 2.6 collective-permute-start.4
  314.8 3.0 collective-permute-start.3
  317.8 1.4 collective-permute-done.4
  319.2 2.3 collective-permute-done.3
  321.6 0.2 copy.56
  321.8 0.2 copy.51
  322.0 0.3 fusion.18
  322.4 0.3 convolution_convert_fusion.2
  322.7 4.6 %convolution_convert_fusion = bf16[128,5120]{1,0:T(8,128)(2,1)} fusion(bf16[128,384]{0,1:T(8,128)(2,1)S(1)} %bitcast.137, bf16[384,5120]{0,1:T(8,128)(2,1)} %all-gather.15.cloned.1.call-done), kind=kOutput, calls=%fused_computation | convolution fusion | flops 503971840 | bytes 5341184 | tf_op jit(solution)/shard_map/dot_general | solution.py:156
  327.4 23.7 %reduce-scatter.5.cloned.1.call-done = bf16[128,2560]{1,0:T(8,128)(2,1)} async-done(((bf16[128,5120]{1,0:T(8,128)(2,1)}), bf16[128,2560]{1,0:T(8,128)(2,1)}) %reduce-scatter.5.cloned.1.call-update) | async-done | bytes 655376 | tf_op jit(solution)/shard_map/reduce_scatter | solution.py:157
  351.1 2.5 fusion.11
  (59 shorter events, 1.4 us)
Async XLA Ops:
  7.2 28.8 %all-gather.7.cloned.1.call-start = ((), (), s32[]{:S(2)}) async-start(), calls=%async_computation.2 | async-start | bytes 1966080 | tf_op jit(solution)/shard_map/all_gather | solution.py:153
  7.9 79.5 %all-gather.13.cloned.1.call-start = ((), (), s32[]{:S(2)}) async-start(), calls=%async_computation.5 | async-start | bytes 4177920 | tf_op jit(solution)/shard_map/all_gather | solution.py:71
  8.6 129.0 %all-gather.9.cloned.1.call-start = ((), (), s32[]{:S(2)}) async-start(), calls=%async_computation.3 | async-start | bytes 4177920 | tf_op jit(solution)/shard_map/all_gather | solution.py:72
  9.4 178.3 %all-gather.11.cloned.1.call-start = ((), (), s32[]{:S(2)}) async-start(), calls=%async_computation.4 | async-start | bytes 4177920 | tf_op jit(solution)/shard_map/all_gather | solution.py:73
  10.0 228.1 %all-gather.15.cloned.1.call-start = ((), (), s32[]{:S(2)}) async-start(), calls=%async_computation.6 | async-start | bytes 4177920 | tf_op jit(solution)/shard_map/all_gather | solution.py:75
  10.5 254.2 %reduce-scatter.3.cloned.1.call-start = ((), (), s32[]{:S(2)}) async-start(), calls=%async_computation.7 | async-start | bytes 1966080 | tf_op jit(solution)/shard_map/reduce_scatter | solution.py:157
  35.9 3.5 copy-start.3
  143.9 3.7 %copy-start.1 = (bf16[384,5120]{1,0:T(8,128)(2,1)S(1)}, bf16[384,5120]{1,0:T(8,128)(2,1)}, u32[]{:S(2)}) copy-start(bf16[384,5120]{1,0:T(8,128)(2,1)} %copy.40) | copy-start | bytes 11796484
  190.7 7.0 %collective-permute-start.1 = (bf16[128,2,384]{2,0,1:T(8,128)(2,1)S(1)}, bf16[128,2,384]{2,0,1:T(8,128)(2,1)S(1)}, u32[]{:S(2)}, u32[]{:S(2)}) collective-permute-start(bf16[128,2,384]{2,0,1:T(8,128)(2,1)S(1)} %pad_maximum_fusion.3), channel_id=1, source_target_pairs={{2,0},{4,2},{6,4},{8,6},{10,8},{12,10},{14,12},{16,14},{18,16},{20... | collective-permute-start | bytes 589832 | tf_op jit(solution)/shard_map/ppermute | solution.py:22
  192.9 9.1 %collective-permute-start = (bf16[128,2,384]{2,0,1:T(8,128)(2,1)S(1)}, bf16[128,2,384]{2,0,1:T(8,128)(2,1)S(1)}, u32[]{:S(2)}, u32[]{:S(2)}) collective-permute-start(bf16[128,2,384]{2,0,1:T(8,128)(2,1)S(1)} %pad_maximum_fusion.3), channel_id=1, source_target_pairs={{0,2},{2,4},{4,6},{6,8},{8,10},{10,12},{12,14},{14,16},{16,18},{18... | collective-permute-start | bytes 589832 | tf_op jit(solution)/shard_map/ppermute | solution.py:20
  238.1 4.7 %copy-start.6 = (s32[2]{0:T(128)S(1)}, s32[2]{0:T(128)}, u32[]{:S(2)}) copy-start(s32[2]{0:T(128)} %param.18) | copy-start | bytes 28
  238.1 4.7 %copy-start.7 = (f32[65]{0:T(128)S(1)}, f32[65]{0:T(128)}, u32[]{:S(2)}) copy-start(f32[65]{0:T(128)} %param.17) | copy-start | bytes 784
  238.1 26.7 %copy-start.4 = (bf16[128,2560]{1,0:T(8,128)(2,1)S(1)}, bf16[128,2560]{1,0:T(8,128)(2,1)}, u32[]{:S(2)}) copy-start(bf16[128,2560]{1,0:T(8,128)(2,1)} %param.10) | copy-start | bytes 1966084
  242.7 31.9 %copy-start.5 = (bf16[64,2560]{1,0:T(8,128)(2,1)S(1)}, bf16[64,2560]{1,0:T(8,128)(2,1)}, u32[]{:S(2)}) copy-start(bf16[64,2560]{1,0:T(8,128)(2,1)} %param.11) | copy-start | bytes 983044
  242.7 56.7 %all-gather.17.cloned.1.call-start = ((), (), s32[]{:S(2)}) async-start(), calls=%async_computation.8 | async-start | bytes 1966080 | tf_op jit(solution)/shard_map/all_gather | solution.py:153
  266.2 8.4 %collective-permute-start.2 = (bf16[64,2560]{1,0:T(8,128)(2,1)S(1)}, bf16[64,2560]{1,0:T(8,128)(2,1)S(1)}, u32[]{:S(2)}, u32[]{:S(2)}) collective-permute-start(bf16[64,2560]{1,0:T(8,128)(2,1)S(1)} %get-tuple-element.7), channel_id=1, source_target_pairs={{2,0},{4,2},{6,4},{8,6},{10,8},{12,10},{14,12},{16,14},{18,16},{20... | collective-permute-start | bytes 983048 | tf_op jit(solution)/shard_map/ppermute | solution.py:32
  275.6 75.5 %reduce-scatter.5.cloned.1.call-start = ((), (), s32[]{:S(2)}) async-start(), calls=%async_computation.9 | async-start | bytes 1966080 | tf_op jit(solution)/shard_map/reduce_scatter | solution.py:157
  299.4 5.5 %copy-start.2 = (bf16[384,5120]{1,0:T(8,128)(2,1)S(1)}, bf16[384,5120]{1,0:T(8,128)(2,1)}, u32[]{:S(2)}) copy-start(bf16[384,5120]{1,0:T(8,128)(2,1)} %copy.40) | copy-start | bytes 11796484
  304.9 2.1 copy-start
  312.2 7.0 %collective-permute-start.4 = (bf16[128,2,384]{2,0,1:T(8,128)(2,1)S(1)}, bf16[128,2,384]{2,0,1:T(8,128)(2,1)S(1)}, u32[]{:S(2)}, u32[]{:S(2)}) collective-permute-start(bf16[128,2,384]{2,0,1:T(8,128)(2,1)S(1)} %pad_maximum_fusion.4), channel_id=1, source_target_pairs={{2,0},{4,2},{6,4},{8,6},{10,8},{12,10},{14,12},{16,14},{18,16},{20... | collective-permute-start | bytes 589832 | tf_op jit(solution)/shard_map/ppermute | solution.py:22
  314.8 6.7 %collective-permute-start.3 = (bf16[128,2,384]{2,0,1:T(8,128)(2,1)S(1)}, bf16[128,2,384]{2,0,1:T(8,128)(2,1)S(1)}, u32[]{:S(2)}, u32[]{:S(2)}) collective-permute-start(bf16[128,2,384]{2,0,1:T(8,128)(2,1)S(1)} %pad_maximum_fusion.4), channel_id=1, source_target_pairs={{0,2},{2,4},{4,6},{6,8},{8,10},{10,12},{12,14},{14,16},{16,18},{18... | collective-permute-start | bytes 589832 | tf_op jit(solution)/shard_map/ppermute | solution.py:20
Sparse Core Ops, SparseCore 0:
  9.5 26.3 all-gather.6
  38.2 49.1 all-gather.12
  89.7 47.8 all-gather.8
  139.8 47.8 all-gather.10
  189.8 48.2 all-gather.14
  242.9 21.8 reduce-scatter.2
  275.7 23.6 all-gather.16
  327.4 23.6 reduce-scatter.4
where the time goes:
time: 362 us; the launch traced here: 360 us
  waiting for transfers between devices  272 us (75%)
  matrix products  27.8 us (8%)
  other arithmetic  16.7 us (5%)
  local copies, waits for them, and re-layouts  14.8 us (4%)
  between operations  14.5 us (4%)
  starting transfers between devices  14.2 us (4%)
    all_gather x1, waiting for transfers between devices, per_device(): lax.all_gather(w_query, 'frame', axis=0, tiled=True)  47.4 us
    reduce_scatter x2, waiting for transfers between devices, reduced(): lax.psum_scatter(product.astype(jnp.bfloat16), 'head', scatter_dimension=...  45.4 us
    all_gather x2, waiting for transfers between devices, gathered(): return lax.all_gather(queue_state, 'head', axis=1, tiled=True)  44.6 us
    all_gather x1, waiting for transfers between devices, per_device(): lax.all_gather(w_key, 'frame', axis=0, tiled=True)  43.9 us
    all_gather x1, waiting for transfers between devices, per_device(): lax.all_gather(w_value, 'frame', axis=0, tiled=True)  38 us
    all_gather x1, waiting for transfers between devices, per_device(): output_full = lax.all_gather(w_output, 'frame', axis=1, tiled=True)  34.9 us
    dot_general x2, matrix products, reduced(): product = jnp.dot(attended, output_full, preferred_element_type=jnp.float32)  9.17 us
  transfers between devices with their start and end apart: 13, of which 13 were waited for; matrix products, arithmetic and copies ran while one was open for 9% of the time, Pallas kernels for 0%

commit v1 on v0

v1 whole, which is shorter than its diff:
```python
import functools
import math

import jax
import jax.numpy as jnp
from jax import lax
from jax.experimental import pallas as pl
from jax.experimental.pallas import tpu as pltpu
from jax.sharding import PartitionSpec as P

HEAD_SIZE = 128
REACH = 2
MESH = pl.DeviceIdType.MESH
F32 = jnp.float32
BF16 = jnp.bfloat16


def kernel(
    F,
    H,
    queue_ref,
    noise_ref,
    wk_ref,
    wv_ref,
    wq_ref,
    wo_ref,
    mod_ref,
    sig_ref,
    cos_ref,
    sin_ref,
    vel_ref,
    out_ref,
    W,
    WO,
    ZA,
    ZB,
    MOD,
    NX,
    QB,
    KB,
    VB,
    ATT,
    own_sem,
    w_recv,
    w_up,
    w_dn,
    w_x,
    w_sib,
    o_yrecv,
    o_ysend,
    o_recv,
    o_up,
    o_dn,
    o_x,
    o_sib,
    q_recv,
    q_send,
    n_recv,
    n_send,
    a_recv,
    a_send,
    b_recv,
    b_send,
    k_recv,
    k_send,
    v_recv,
    v_send,
    t_recv,
    t_send,
):
    f = lax.axis_index("frame")
    h = lax.axis_index("head")
    Z = F // 4
    zs = Z // H
    z = f // 4
    x = (f // 2) % 2
    c = f % 2
    R, inner = wk_ref.shape
    T, slab = queue_ref.shape
    half = T // 2
    NC = 640
    chunks = slab // NC
    heads = inner // HEAD_SIZE
    pending = []

    def fid(zz, xx, cc):
        return (zz * 2 + xx) * 2 + cc

    def head_at(step):
        return (h + step) % H

    def send(src, dst, ssem, rsem, to_f, to_h, when=None):
        def make():
            return pltpu.make_async_remote_copy(
                src_ref=src,
                dst_ref=dst,
                send_sem=ssem,
                recv_sem=rsem,
                device_id=(to_f, to_h),
                device_id_type=MESH,
            )

        guarded(when, lambda: make().start())
        pending.append((when, lambda: make().wait_send()))

    def guarded(when, action):
        if when is None:
            action()
        else:
            pl.when(when)(action)

    def arrived(dst, rsem, when=None):
        guarded(
            when,
            lambda: pltpu.make_async_remote_copy(
                src_ref=dst,
                dst_ref=dst,
                send_sem=rsem,
                recv_sem=rsem,
                device_id=(fid(z, x, 1 - c), h),
                device_id_type=MESH,
            ).wait_recv(),
        )

    barrier = pltpu.get_barrier_semaphore()
    greet = [
        (z < Z - 1, f + 4, h),
        (z > 0, f - 4, h),
        (None, fid(z, 1 - x, c), h),
        (None, fid(z, x, 1 - c), h),
        (f < F - 1, f + 1, h),
        (f > 0, f - 1, h),
    ]
    for step in range(1, H):
        greet += [
            (None, f, head_at(step)),
            (f < F - 1, f + 1, head_at(step)),
            (f > 0, f - 1, head_at(step)),
        ]
    for when, to_f, to_h in greet:
        guarded(
            when,
            lambda to_f=to_f, to_h=to_h: pl.semaphore_signal(
                barrier, inc=1, device_id=(to_f, to_h), device_id_type=MESH
            ),
        )
    always = sum(when is None for when, _, _ in greet)
    sometimes = sum(when.astype(jnp.int32) for when, _, _ in greet if when is not None)
    pl.semaphore_wait(barrier, always + sometimes)

    shards = [wk_ref, wv_ref, wq_ref]

    def slot(m, zz, xx, cc):
        return W.at[m, pl.ds(pl.multiple_of(fid(zz, xx, cc) * R, 32), R), :]

    def spread_w(m, zz, src, up, down):
        dst = slot(m, zz, x, c)
        rsem = w_recv.at[m, fid(zz, x, c)]
        if up:
            send(src, dst, w_up.at[m, zz], rsem, f + 4, h, when=up[0])
        if down:
            send(src, dst, w_dn.at[m, zz], rsem, f - 4, h, when=down[0])
        send(src, dst, w_x.at[m, zz], rsem, fid(z, 1 - x, c), h, when=(up or down)[1])
        send(src, dst, w_sib.at[m, zz, x], rsem, fid(z, x, 1 - c), h, when=(up or down)[1])

    def w_own(m):
        spread_w(m, z, shards[m], (z < Z - 1, None), (z > 0, None))

    def w_along(m, d):
        below = z - d >= 0
        arrived(slot(m, z - d, x, c), w_recv.at[m, fid(z - d, x, c)], when=below)
        spread_w(m, z - d, slot(m, z - d, x, c), (below & (z < Z - 1), below), None)
        above = z + d <= Z - 1
        arrived(slot(m, z + d, x, c), w_recv.at[m, fid(z + d, x, c)], when=above)
        spread_w(m, z + d, slot(m, z + d, x, c), None, (above & (z > 0), above))

    def w_across(m, d):
        for zz, ok in ((z - d, z - d >= 0), (z + d, z + d <= Z - 1))[: 2 if d else 1]:
            ok = ok if d else None
            piece = slot(m, zz, 1 - x, c)
            rsem = w_recv.at[m, fid(zz, 1 - x, c)]
            arrived(piece, rsem, when=ok)
            send(piece, piece, w_sib.at[m, zz, 1 - x], rsem, fid(z, x, 1 - c), h, when=ok)

    def w_last(m):
        for zz in range(Z):
            for xx in range(2):
                arrived(slot(m, zz, xx, 1 - c), w_recv.at[m, fid(zz, xx, 1 - c)])
        pltpu.make_async_copy(shards[m], slot(m, z, x, c), own_sem.at[m]).wait()

    def o_slot(g, j, xx, cc):
        return WO.at[g, pl.ds(pl.multiple_of(fid(j, xx, cc) * R, 32), R), :]

    mine = z // zs
    here = mine == h
    rank = z - mine * zs

    def o_turn(i):
        j = jnp.where(z <= h * zs, i, zs - 1 - i)
        zz = h * zs + j
        for g in range(H):
            piece = o_slot(g, j, x, c)
            rsem = o_recv.at[g, fid(j, x, c)]
            arrived(piece, rsem, when=zz != z)
            arrived(piece, o_yrecv.at[g], when=(zz == z) & (h != g))
            send(piece, piece, o_up.at[g, j], rsem, f + 4, h, when=(zz <= z) & (z < Z - 1))
            send(piece, piece, o_dn.at[g, j], rsem, f - 4, h, when=(zz >= z) & (z > 0))
            send(piece, piece, o_x.at[g, j], rsem, fid(z, 1 - x, c), h)
            send(piece, piece, o_sib.at[g, j, x], rsem, fid(z, x, 1 - c), h)

    def o_across(i):
        j = jnp.where(z <= h * zs, i, zs - 1 - i)
        for g in range(H):
            piece = o_slot(g, j, 1 - x, c)
            rsem = o_recv.at[g, fid(j, 1 - x, c)]
            arrived(piece, rsem)
            send(piece, piece, o_sib.at[g, j, 1 - x], rsem, fid(z, x, 1 - c), h)

    def o_last():
        for g in range(H):
            for j in range(zs):
                for xx in range(2):
                    arrived(o_slot(g, j, xx, 1 - c), o_recv.at[g, fid(j, xx, 1 - c)])

    w_own(0)
    for step in range(1, H):
        send(queue_ref, ZA.at[h], q_send.at[step], q_recv.at[h], f, head_at(step))
    queue_own = pltpu.make_async_copy(queue_ref, ZA.at[h], own_sem.at[4])
    queue_own.start()
    for m in range(3):
        pltpu.make_async_copy(shards[m], slot(m, z, x, c), own_sem.at[m]).start()
    o_own = lambda: pltpu.make_async_copy(wo_ref, o_slot(h, rank, x, c), own_sem.at[3])
    guarded(here, lambda: o_own().start())
    guarded(here, lambda: o_own().wait())
    send(wo_ref, o_slot(h, rank, x, c), o_ysend.at[0], o_yrecv.at[h], f, mine, when=mine != h)
    last = f == F - 1
    noise_own = lambda: pltpu.make_async_copy(
        noise_ref, ZB.at[h, pl.ds(half, half), :], own_sem.at[5]
    )
    guarded(last, lambda: noise_own().start())
    for step in range(1, H):
        send(
            noise_ref,
            ZB.at[h, pl.ds(half, half), :],
            n_send.at[step],
            n_recv.at[h],
            f,
            head_at(step),
            when=last,
        )
    for s in range(2):

        @pl.when(f == 0)
        def _(s=s):
            KB[s, :T] = jnp.zeros((T, inner), BF16)
            VB[s, :T] = jnp.zeros((T, inner), BF16)

        @pl.when(last)
        def _(s=s):
            KB[s, 2 * T :] = jnp.zeros((T, inner), BF16)
            VB[s, 2 * T :] = jnp.zeros((T, inner), BF16)

    def modulate(src):
        rows = 16
        for b in range(2):

            def body(i, carry, b=b):
                at = pl.ds(pl.multiple_of(b * half + i * rows, rows), rows)
                wide = [src[g, at, :].astype(F32) for g in range(H)]
                total = sum(jnp.sum(w, axis=-1, keepdims=True) for w in wide)
                mean = total / (H * slab)
                wide = [w - mean for w in wide]
                square = sum(jnp.sum(w * w, axis=-1, keepdims=True) for w in wide)
                scale_by = lax.rsqrt(square / (H * slab) + 1e-06)
                for g in range(H):
                    shift = mod_ref[pl.ds((b * 3) * H + g, 1), :]
                    scale = mod_ref[pl.ds((b * 3 + 1) * H + g, 1), :]
                    MOD[g, at, :] = (wide[g] * scale_by * (1.0 + scale) + shift).astype(BF16)
                return carry

            lax.fori_loop(0, half // rows, body, 0)

    depth = 1280 if slab % 1280 == 0 else slab

    def project(m):
        total = jnp.zeros((T, inner), F32)
        for g in range(H):

            def body(i, acc, g=g):
                at = pl.multiple_of(i * depth, 128)
                return acc + jnp.dot(
                    MOD[g, :, pl.ds(at, depth)],
                    W[m, pl.ds(g * slab + at, depth), :],
                    preferred_element_type=F32,
                )

            total = lax.fori_loop(0, slab // depth, body, total)
        return total

    def rotated(full):
        parts = []
        for i in range(heads):
            one = full[:, i * HEAD_SIZE : (i + 1) * HEAD_SIZE]
            one = one * lax.rsqrt(jnp.mean(one * one, axis=-1, keepdims=True) + 1e-06)
            turned = pltpu.roll(one, HEAD_SIZE // 2, 1)
            parts.append((one * cos_ref[...] + turned * sin_ref[...]).astype(BF16))
        return parts

    def keys(s):
        for i, part in enumerate(rotated(project(0))):
            KB[s, T : 2 * T, i * HEAD_SIZE : (i + 1) * HEAD_SIZE] = part
        halo(KB, s, k_send, k_recv)

    def values(s):
        VB[s, T : 2 * T, :] = project(1).astype(BF16)
        halo(VB, s, v_send, v_recv)

    def halo(buf, s, ssem, rsem):
        mid = buf.at[s, pl.ds(T, T), :]
        send(mid, buf.at[s, pl.ds(0, T), :], ssem.at[s, 0], rsem.at[s, 0], f + 1, h, when=f < F - 1)
        send(mid, buf.at[s, pl.ds(2 * T, T), :], ssem.at[s, 1], rsem.at[s, 1], f - 1, h, when=f > 0)

    def queries(s):
        for i, part in enumerate(rotated(project(2))):
            QB[:, i * HEAD_SIZE : (i + 1) * HEAD_SIZE] = part

    def attend(s):
        for buf, rsem in ((KB, k_recv), (VB, v_recv)):
            arrived(buf.at[s, pl.ds(0, T), :], rsem.at[s, 0], when=f > 0)
            arrived(buf.at[s, pl.ds(2 * T, T), :], rsem.at[s, 1], when=f < F - 1)
        shape = (T, 3 * T)
        qb = lax.broadcasted_iota(jnp.int32, shape, 0) // half
        kb = lax.broadcasted_iota(jnp.int32, shape, 1) // half - 2
        near = (kb - qb <= REACH) & (qb - kb <= REACH)
        near = near & (kb + 2 * f >= 0) & (kb + 2 * f < 2 * F)
        for i in range(heads):
            cols = slice(i * HEAD_SIZE, (i + 1) * HEAD_SIZE)
            scores = lax.dot_general(
                QB[:, cols], KB[s, :, cols], (((1,), (1,)), ((), ())), preferred_element_type=F32
            )
            raised = jnp.where(near, jnp.exp(scores * (1.0 / math.sqrt(HEAD_SIZE))), 0.0)
            weights = raised / jnp.sum(raised, axis=-1, keepdims=True)
            ATT[s, h, :, cols] = jnp.dot(
                weights.astype(BF16), VB[s, :, cols], preferred_element_type=F32
            ).astype(BF16)
        for step in range(1, H):
            send(ATT.at[s, h], ATT.at[s, h], t_send.at[s, step], t_recv.at[s, h], f, head_at(step))

    def attended_all(s):
        for step in range(1, H):
            g = head_at(step)
            arrived(ATT.at[s, g], t_recv.at[s, g])

    def advance(s, src):
        for n in range(chunks):
            cols = slice(n * NC, (n + 1) * NC)
            mixed = None
            for g in range(H):
                product = lax.dot_general(
                    ATT[s, g],
                    WO[g, cols, :],
                    (((1,), (1,)), ((), ())),
                    preferred_element_type=F32,
                )
                product = product.astype(BF16).astype(F32)
                mixed = product if mixed is None else mixed + product
            for b in range(2):
                rows = slice(b * half, (b + 1) * half)
                base = src[h, rows, cols].astype(F32)
                gate = mod_ref[pl.ds((b * 3 + 2) * H + h, 1), cols]
                layer_out = base + gate * mixed[rows]
                following = (base + sig_ref[b : b + 1, 0:1] * layer_out).astype(BF16)
                if s == 1:
                    vel_ref[rows, cols] = layer_out.astype(BF16)
                    out_ref[rows, cols] = following
                elif b == 0:
                    NX[:, cols] = following
                else:
                    ZB[h, :half, cols] = following
            if s == 0:
                at = pl.ds(n * NC, NC)
                low = ZB.at[h, pl.ds(0, half), at]
                high = ZB.at[h, pl.ds(half, half), at]
                for step in range(H):
                    to_h = head_at(step)
                    if step:
                        send(low, low, a_send.at[step, n], a_recv.at[h, n], f, to_h)
                    send(
                        NX.at[:, at],
                        high,
                        b_send.at[step, n],
                        b_recv.at[h, n],
                        f - 1,
                        to_h,
                        when=f > 0,
                    )

    def second_state():
        for step in range(H):
            g = head_at(step)
            for n in range(chunks):
                at = pl.ds(n * NC, NC)
                if step:
                    arrived(ZB.at[g, pl.ds(0, half), at], a_recv.at[g, n])
                arrived(ZB.at[g, pl.ds(half, half), at], b_recv.at[g, n], when=f < F - 1)
            if step:
                arrived(ZB.at[g, pl.ds(half, half), :], n_recv.at[g], when=last)
        guarded(last, lambda: noise_own().wait())

    w_along(0, 1)
    w_own(1)
    w_across(0, 0)
    for d in range(2, Z):
        w_along(0, d)
        w_across(0, d - 1)
    w_along(1, 1)
    for step in range(1, H):
        g = head_at(step)
        arrived(ZA.at[g], q_recv.at[g])
    queue_own.wait()
    modulate(ZA)
    w_across(0, Z - 1)
    w_own(2)
    w_last(0)
    w_across(1, 0)
    keys(0)
    for d in range(2, Z):
        w_along(1, d)
        w_across(1, d - 1)
    w_along(2, 1)
    w_across(1, Z - 1)
    w_last(1)
    w_across(2, 0)
    values(0)
    for d in range(2, Z):
        w_along(2, d)
        w_across(2, d - 1)
    o_turn(0)
    w_across(2, Z - 1)
    w_last(2)
    queries(0)
    o_across(0)
    for i in range(1, zs):
        o_turn(i)
    attend(0)
    for i in range(1, zs):
        o_across(i)
    o_last()
    attended_all(0)
    advance(0, ZA)
    second_state()
    modulate(ZB)
    keys(1)
    values(1)
    queries(1)
    attend(1)
    attended_all(1)
    advance(1, ZB)
    for when, action in pending:
        guarded(when, action)


def per_device(
    queue,
    noise_block,
    w_query,
    w_key,
    w_value,
    w_output,
    mod_table,
    sigma_table,
    timestep_index,
    block_position,
):
    F = lax.axis_size("frame")
    H = lax.axis_size("head")
    T, slab = queue.shape
    blocks = timestep_index.shape[0]
    half = T // blocks
    R, inner = w_key.shape
    Z = F // 4
    zs = Z // H
    chunks = slab // 640
    modulation = jnp.concatenate(
        [lax.dynamic_slice_in_dim(mod_table, timestep_index[b], 1, 0) for b in range(blocks)]
    ).reshape(blocks * 3 * H, slab)
    sigma_step = jnp.stack(
        [
            lax.dynamic_index_in_dim(sigma_table, timestep_index[b] + 1, 0, False)
            - lax.dynamic_index_in_dim(sigma_table, timestep_index[b], 0, False)
            for b in range(blocks)
        ]
    )
    sigma_rows = jnp.broadcast_to(sigma_step[:, None], (blocks, 128))
    half_size = HEAD_SIZE // 2
    freqs = 10000.0 ** (-jnp.arange(half_size, dtype=F32) / half_size)
    angles = block_position.astype(F32)[:, None] * freqs[None, :]
    cosine, sine = jnp.cos(angles), jnp.sin(angles)
    cosine = jnp.repeat(jnp.concatenate([cosine, cosine], axis=-1), half, axis=0)
    sine = jnp.repeat(jnp.concatenate([-sine, sine], axis=-1), half, axis=0)
    dma = pltpu.SemaphoreType.DMA
    vmem = pl.BlockSpec(memory_space=pltpu.VMEM)
    hbm = pl.BlockSpec(memory_space=pl.ANY)
    out = jax.ShapeDtypeStruct((T, slab), BF16)
    return pl.pallas_call(
        functools.partial(kernel, F, H),
        out_shape=(out, out),
        in_specs=[hbm] * 6 + [vmem] * 4,
        out_specs=(vmem, vmem),
        scratch_shapes=[
            pltpu.VMEM((3, F * R, inner), BF16),
            pltpu.VMEM((H, 4 * zs * R, inner), BF16),
            pltpu.VMEM((H, T, slab), BF16),
            pltpu.VMEM((H, T, slab), BF16),
            pltpu.VMEM((H, T, slab), BF16),
            pltpu.VMEM((half, slab), BF16),
            pltpu.VMEM((T, inner), BF16),
            pltpu.VMEM((2, 3 * T, inner), BF16),
            pltpu.VMEM((2, 3 * T, inner), BF16),
            pltpu.VMEM((2, H, T, inner), BF16),
            dma((6,)),
            dma((3, F)),
            dma((3, Z)),
            dma((3, Z)),
            dma((3, Z)),
            dma((3, Z, 2)),
            dma((H,)),
            dma((1,)),
            dma((H, 4 * zs)),
            dma((H, zs)),
            dma((H, zs)),
            dma((H, zs)),
            dma((H, zs, 2)),
            dma((H,)),
            dma((H,)),
            dma((H,)),
            dma((H,)),
            dma((H, chunks)),
            dma((H, chunks)),
            dma((H, chunks)),
            dma((H, chunks)),
            dma((2, 2)),
            dma((2, 2)),
            dma((2, 2)),
            dma((2, 2)),
            dma((2, H)),
            dma((2, H)),
        ],
        compiler_params=pltpu.CompilerParams(
            collective_id=0, has_side_effects=True, vmem_limit_bytes=48 * 1024 * 1024
        ),
        cost_estimate=pl.CostEstimate(
            flops=4 * T * H * slab * inner * 4, bytes_accessed=8 * R * inner * 2, transcendentals=0
        ),
    )(
        queue,
        noise_block,
        w_key,
        w_value,
        w_query,
        w_output.T,
        modulation,
        sigma_rows,
        cosine,
        sine,
    )


def solution(mesh):
    in_specs = (
        P("frame", "head"),
        P(None, "head"),
        P("frame", "head"),
        P("frame", "head"),
        P("frame", "head"),
        P("head", "frame"),
        P(),
        P(),
        P("frame"),
        P("frame"),
    )
    out_specs = (P("frame", "head"), P("frame", "head"))
    return jax.shard_map(
        per_device, mesh=mesh, in_specs=in_specs, out_specs=out_specs, check_vma=False
    )
```

time: 362 us -> 172 us (0.48)
  waiting for transfers between devices: 272 us -> 0 us
  Pallas kernels: 0 us -> 145 us
  matrix products: 27.8 us -> 0 us
  other arithmetic: 16.7 us -> 1.05 us
  starting transfers between devices: 14.2 us -> 0 us
    all_gather x6 -> x0, waiting for transfers between devices: 209 us -> none  [the longest x1 47.4 us: per_device(): lax.all_gather(w_query, 'frame', axis=0, tiled=True)]
    pallas_call x0 -> x1, Pallas kernels: none -> 145 us  [per_device(): pl.pallas_call(functools.partial(kernel, F, H), out_shape=(out, out), in_...]
    reduce_scatter x2 -> x0, waiting for transfers between devices: 45.4 us -> none  [reduced(): lax.psum_scatter(product.astype(jnp.bfloat16), 'head', scatter_dimension=...]
    dot_general x13 -> x0, matrix products: 27.8 us -> none  [the longest x2 9.17 us: reduced(): product = jnp.dot(attended, output_full, preferred_element_type=jnp.float32)]
    ppermute x5 -> x0, waiting for transfers between devices: 15 us -> none  [the longest x2 6.54 us: with_halo(): lax.ppermute(tail, axis, [(i, (i + 1) % count) for i in range(ends)])]
    ppermute x5 -> x0, starting transfers between devices: 13.7 us -> none  [the longest x2 6.39 us: with_halo(): lax.ppermute(tail, axis, [(i, (i + 1) % count) for i in range(ends)])]
    dot_general x2 -> x0, local copies, waits for them, and re-layouts: 12.5 us -> none  [the longest x1 6.29 us: attend(): jnp.dot(modulated, query_full, preferred_element_type=jnp.float32)]
    reduce_sum x5 -> x0, other arithmetic: 7.27 us -> none  [the longest x2 3.63 us: attend(): row_var = jnp.mean((wide_rows - row_mean) ** 2, axis=-1, keepdims=True)]
  transfers between devices with their start and end apart: 13 -> 0, of which waited for: 13 -> 0; matrix products, arithmetic and copies ran while one was open for 9% -> 0% of each run, Pallas kernels for 0% -> 0%
where the time goes in v1:
time: 172 us; the launch traced here: 170 us
  Pallas kernels  145 us (84%)
  between operations  12.3 us (7%)
  local copies, waits for them, and re-layouts  11.8 us (7%)
    pallas_call x1, Pallas kernels, per_device(): pl.pallas_call(functools.partial(kernel, F, H), out_shape=(out, out), in_...  145 us
    unnamed x14, local copies, waits for them, and re-layouts  7.5 us

profile of v1, /device:TPU:1, one launch (start us, length us, event | category | flops | bytes accessed | tf_op | source)
XLA Modules:
  0.0 170.1 jit_solution(1188794205166372788)
XLA Ops:
  0.6 0.7 convert_element_type.3
  1.3 1.3 fusion.2
  11.7 1.5 fusion.1
  15.7 0.1 pad_maximum_fusion.3
  15.8 0.1 broadcast_in_dim.6.sig_ref
  15.8 0.1 fusion
  15.9 0.1 pad_maximum_fusion.1
  16.0 1.3 constant_dynamic-slice_fusion.1
  17.3 0.1 pad_maximum_fusion
  17.4 0.1 copy.13
  17.5 0.1 reshape.25.mod_ref
  17.6 0.0 copy-start
  17.6 1.1 copy-done
  18.7 0.0 copy-start.1
  18.7 1.0 copy-done.1
  19.7 0.0 copy-start.2
  19.7 0.9 copy-done.2
  20.6 0.0 copy-start.3
  20.6 0.9 copy-done.3
  21.6 0.0 copy-start.4
  21.6 0.9 copy-done.4
  22.5 0.0 copy-start.5
  22.5 0.9 copy-done.5
  23.4 145.0 %shard_map.113 = (bf16[128,2560]{1,0:T(8,128)(2,1)S(1)}, bf16[128,2560]{1,0:T(8,128)(2,1)S(1)}) custom-call(bf16[128,2560]{1,0:T(8,128)(2,1)S(1)} %copy-done, bf16[64,2560]{1,0:T(8,128)(2,1)S(1)} %copy-done.1, bf16[320,384]{1,0:T(8,128)(2,1)S(1)} %copy-done.2, bf16[320,384]{1,0:T(8,128)(2,1)S(1)} %copy-done.3, bf16[320,384]{1,0:T(8,128)(2,1)S(1)} %copy-done.4, ...), custom_call_target="tpu_custom_call" | custom-call | flops 4026531840 | bytes 1966080 | tf_op jit(solution)/shard_map/pallas_call | solution.py:505
  168.4 0.8 copy.16
  169.3 0.8 copy.17
  (3 shorter events, 0.0 us)
Async XLA Ops:
  17.6 1.1 copy-start
  18.7 1.0 copy-start.1
  19.7 0.9 copy-start.2
  20.6 0.9 copy-start.3
  21.6 0.9 copy-start.4
  22.5 0.9 copy-start.5

commit v2 on v1

--- a/solution.py
+++ b/solution.py
@@ -3,6 +3,7 @@
 
 import jax
 import jax.numpy as jnp
+import numpy as np
 from jax import lax
 from jax.experimental import pallas as pl
 from jax.experimental.pallas import tpu as pltpu
@@ -24,10 +25,11 @@
     wv_ref,
     wq_ref,
     wo_ref,
-    mod_ref,
-    sig_ref,
-    cos_ref,
-    sin_ref,
+    table_ref,
+    freq_ref,
+    sigma_ref,
+    level_ref,
+    pos_ref,
     vel_ref,
     out_ref,
     W,
@@ -40,6 +42,10 @@
     KB,
     VB,
     ATT,
+    table,
+    mod_ref,
+    cos_ref,
+    sin_ref,
     own_sem,
     w_recv,
     w_up,
@@ -223,6 +229,8 @@
                     arrived(o_slot(g, j, xx, 1 - c), o_recv.at[g, fid(j, xx, 1 - c)])
 
     w_own(0)
+    table_own = pltpu.make_async_copy(table_ref, table, own_sem.at[6])
+    table_own.start()
     for step in range(1, H):
         send(queue_ref, ZA.at[h], q_send.at[step], q_recv.at[h], f, head_at(step))
     queue_own = pltpu.make_async_copy(queue_ref, ZA.at[h], own_sem.at[4])
@@ -260,6 +268,24 @@
             KB[s, 2 * T :] = jnp.zeros((T, inner), BF16)
             VB[s, 2 * T :] = jnp.zeros((T, inner), BF16)
 
+    def tables():
+        lane = lax.broadcasted_iota(jnp.int32, (1, HEAD_SIZE), 1)
+        sign = jnp.where(lane < HEAD_SIZE // 2, -1.0, 1.0)
+        for b in range(2):
+            level = level_ref[b]
+            for k in range(3):
+                for g in range(H):
+                    mod_ref[(b * 3 + k) * H + g : (b * 3 + k) * H + g + 1, :] = table[
+                        k, pl.ds(level, 1), g * slab : (g + 1) * slab
+                    ]
+            angles = freq_ref[...] * pos_ref[b].astype(F32)
+            rows = slice(b * half, (b + 1) * half)
+            cos_ref[rows, :] = jnp.broadcast_to(jnp.cos(angles), (half, HEAD_SIZE))
+            sin_ref[rows, :] = jnp.broadcast_to(jnp.sin(angles) * sign, (half, HEAD_SIZE))
+
+    def sigma_step(b):
+        return sigma_ref[level_ref[b] + 1] - sigma_ref[level_ref[b]]
+
     def modulate(src):
         rows = 16
         for b in range(2):
@@ -369,7 +395,7 @@
                 base = src[h, rows, cols].astype(F32)
                 gate = mod_ref[pl.ds((b * 3 + 2) * H + h, 1), cols]
                 layer_out = base + gate * mixed[rows]
-                following = (base + sig_ref[b : b + 1, 0:1] * layer_out).astype(BF16)
+                following = (base + sigma_step(b) * layer_out).astype(BF16)
                 if s == 1:
                     vel_ref[rows, cols] = layer_out.astype(BF16)
                     out_ref[rows, cols] = following
@@ -418,6 +444,8 @@
         g = head_at(step)
         arrived(ZA.at[g], q_recv.at[g])
     queue_own.wait()
+    table_own.wait()
+    tables()
     modulate(ZA)
     w_across(0, Z - 1)
     w_own(2)
@@ -477,35 +505,22 @@
     T, slab = queue.shape
     blocks = timestep_index.shape[0]
     half = T // blocks
+    levels = mod_table.shape[0]
     R, inner = w_key.shape
     Z = F // 4
     zs = Z // H
     chunks = slab // 640
-    modulation = jnp.concatenate(
-        [lax.dynamic_slice_in_dim(mod_table, timestep_index[b], 1, 0) for b in range(blocks)]
-    ).reshape(blocks * 3 * H, slab)
-    sigma_step = jnp.stack(
-        [
-            lax.dynamic_index_in_dim(sigma_table, timestep_index[b] + 1, 0, False)
-            - lax.dynamic_index_in_dim(sigma_table, timestep_index[b], 0, False)
-            for b in range(blocks)
-        ]
-    )
-    sigma_rows = jnp.broadcast_to(sigma_step[:, None], (blocks, 128))
-    half_size = HEAD_SIZE // 2
-    freqs = 10000.0 ** (-jnp.arange(half_size, dtype=F32) / half_size)
-    angles = block_position.astype(F32)[:, None] * freqs[None, :]
-    cosine, sine = jnp.cos(angles), jnp.sin(angles)
-    cosine = jnp.repeat(jnp.concatenate([cosine, cosine], axis=-1), half, axis=0)
-    sine = jnp.repeat(jnp.concatenate([-sine, sine], axis=-1), half, axis=0)
+    freqs = 10000.0 ** (-np.arange(HEAD_SIZE // 2) / (HEAD_SIZE // 2))
+    freqs = jnp.asarray(np.concatenate([freqs, freqs])[None, :].astype(np.float32))
     dma = pltpu.SemaphoreType.DMA
     vmem = pl.BlockSpec(memory_space=pltpu.VMEM)
+    smem = pl.BlockSpec(memory_space=pltpu.SMEM)
     hbm = pl.BlockSpec(memory_space=pl.ANY)
     out = jax.ShapeDtypeStruct((T, slab), BF16)
     return pl.pallas_call(
         functools.partial(kernel, F, H),
         out_shape=(out, out),
-        in_specs=[hbm] * 6 + [vmem] * 4,
+        in_specs=[hbm] * 7 + [vmem] + [smem] * 3,
         out_specs=(vmem, vmem),
         scratch_shapes=[
             pltpu.VMEM((3, F * R, inner), BF16),
@@ -518,7 +533,11 @@
             pltpu.VMEM((2, 3 * T, inner), BF16),
             pltpu.VMEM((2, 3 * T, inner), BF16),
             pltpu.VMEM((2, H, T, inner), BF16),
-            dma((6,)),
+            pltpu.VMEM((3, levels, H * slab), F32),
+            pltpu.VMEM((blocks * 3 * H, slab), F32),
+            pltpu.VMEM((T, HEAD_SIZE), F32),
+            pltpu.VMEM((T, HEAD_SIZE), F32),
+            dma((7,)),
             dma((3, F)),
             dma((3, Z)),
             dma((3, Z)),
@@ -547,7 +566,7 @@
             dma((2, H)),
         ],
         compiler_params=pltpu.CompilerParams(
-            collective_id=0, has_side_effects=True, vmem_limit_bytes=48 * 1024 * 1024
+            collective_id=0, has_side_effects=True, vmem_limit_bytes=62 * 1024 * 1024
         ),
         cost_estimate=pl.CostEstimate(
             flops=4 * T * H * slab * inner * 4, bytes_accessed=8 * R * inner * 2, transcendentals=0
@@ -559,10 +578,11 @@
         w_value,
         w_query,
         w_output.T,
-        modulation,
-        sigma_rows,
-        cosine,
-        sine,
+        jnp.transpose(mod_table, (1, 0, 2)),
+        freqs,
+        sigma_table,
+        timestep_index,
+        block_position,
     )
 
 

time: 172 us -> 154 us (0.90)
  between operations: 12.3 us -> 0.64 us
  local copies, waits for them, and re-layouts: 11.8 us -> 3.93 us
  Pallas kernels: 145 us -> 147 us
    unnamed x14 -> x2, local copies, waits for them, and re-layouts: 7.5 us -> 3.93 us
    dynamic_slice x2 -> x0, local copies, waits for them, and re-layouts: 2.74 us -> none  [the longest x1 1.47 us: per_device(): lax.dynamic_index_in_dim(sigma_table, timestep_index[b], 0, False)]
    pallas_call x1, Pallas kernels: 145 us -> 147 us  [per_device(): pl.pallas_call(functools.partial(kernel, F, H), out_shape=(out, out), in_...]
where the time goes in v2:
time: 154 us; the launch traced here: 152 us
  Pallas kernels  147 us (95%)
  local copies, waits for them, and re-layouts  3.93 us (3%)
    pallas_call x1, Pallas kernels, per_device(): pl.pallas_call(functools.partial(kernel, F, H), out_shape=(out, out), in_...  147 us
    unnamed x2, local copies, waits for them, and re-layouts  3.93 us

profile of v2, /device:TPU:1, one launch (start us, length us, event | category | flops | bytes accessed | tf_op | source)
XLA Modules:
  0.0 152.0 jit_solution(16361600580052139456)
XLA Ops:
  0.6 147.4 %shard_map.122 = (bf16[128,2560]{1,0:T(8,128)(2,1)}, bf16[128,2560]{1,0:T(8,128)(2,1)}) custom-call(bf16[128,2560]{1,0:T(8,128)(2,1)} %queue_ref.1, bf16[64,2560]{1,0:T(8,128)(2,1)} %noise_ref.1, bf16[320,384]{1,0:T(8,128)(2,1)} %wk_ref.1, bf16[320,384]{1,0:T(8,128)(2,1)} %wv_ref.1, bf16[320,384]{1,0:T(8,128)(2,1)} %wq_ref.1, bf16[320,384]{1,0:T(8,128)(2,1)} %bitcast.3, ...), custom_call_target="tpu_custom_call" | custom-call | flops 4026531840 | bytes 1966080 | tf_op jit(solution)/shard_map/pallas_call | solution.py:520
  148.1 2.0 %copy.15 = bf16[128,2560]{1,0:T(8,128)(2,1)} copy(bf16[128,2560]{1,0:T(8,128)(2,1)} %get-tuple-element.4) | data formatting | bytes 1310720
  150.0 2.0 %copy.16 = bf16[128,2560]{1,0:T(8,128)(2,1)} copy(bf16[128,2560]{1,0:T(8,128)(2,1)} %get-tuple-element.5) | data formatting | bytes 1310720

commit v3 on v2

v3 whole, which is shorter than its diff:
```python
import functools
import math

import jax
import jax.numpy as jnp
import numpy as np
from jax import lax
from jax.experimental import pallas as pl
from jax.experimental.pallas import tpu as pltpu
from jax.sharding import PartitionSpec as P

HEAD_SIZE = 128
REACH = 2
MESH = pl.DeviceIdType.MESH
F32 = jnp.float32
BF16 = jnp.bfloat16


def kernel(
    F,
    H,
    queue_ref,
    noise_ref,
    wk_ref,
    wv_ref,
    wq_ref,
    wo_ref,
    table_ref,
    freq_ref,
    sigma_ref,
    level_ref,
    pos_ref,
    vel_ref,
    out_ref,
    W,
    ZL,
    ZA,
    ZB,
    MOD,
    NX,
    QB,
    KB,
    VB,
    ATT,
    PO,
    PS,
    PR,
    ST,
    table,
    mod_ref,
    cos_ref,
    sin_ref,
    own_sem,
    z_recv,
    z_up,
    z_dn,
    y_send,
    y_recv,
    x_send,
    x_recv,
    s_send,
    s_recv,
    l_sem,
    b_recv,
    b_send,
    k_recv,
    k_send,
    v_recv,
    v_send,
    t_recv,
    t_send,
    p_recv,
    p_send,
    st_recv,
    st_send,
):
    f = lax.axis_index("frame")
    h = lax.axis_index("head")
    Z = F // 4
    zs = Z // H
    z = f // 4
    x = (f // 2) % 2
    c = f % 2
    R, inner = wk_ref.shape
    T, slab = queue_ref.shape
    half = T // 2
    NC = 640
    chunks = slab // NC
    heads = inner // HEAD_SIZE
    pending = []

    def fid(zz, xx, cc):
        return (zz * 2 + xx) * 2 + cc

    def head_at(step):
        return (h + step) % H

    def send(src, dst, ssem, rsem, to_f, to_h, when=None):
        def make():
            return pltpu.make_async_remote_copy(
                src_ref=src,
                dst_ref=dst,
                send_sem=ssem,
                recv_sem=rsem,
                device_id=(to_f, to_h),
                device_id_type=MESH,
            )

        guarded(when, lambda: make().start())
        pending.append((when, lambda: make().wait_send()))

    def guarded(when, action):
        if when is None:
            action()
        else:
            pl.when(when)(action)

    def arrived(dst, rsem, when=None):
        guarded(
            when,
            lambda: pltpu.make_async_remote_copy(
                src_ref=dst,
                dst_ref=dst,
                send_sem=rsem,
                recv_sem=rsem,
                device_id=(fid(z, x, 1 - c), h),
                device_id_type=MESH,
            ).wait_recv(),
        )

    barrier = pltpu.get_barrier_semaphore()
    greet = [
        (z < Z - 1, f + 4, h),
        (z > 0, f - 4, h),
        (None, fid(z, 1 - x, c), h),
        (None, fid(z, x, 1 - c), h),
        (f < F - 1, f + 1, h),
        (f > 0, f - 1, h),
    ]
    for step in range(1, H):
        greet.append((None, f, head_at(step)))
    for when, to_f, to_h in greet:
        guarded(
            when,
            lambda to_f=to_f, to_h=to_h: pl.semaphore_signal(
                barrier, inc=1, device_id=(to_f, to_h), device_id_type=MESH
            ),
        )
    always = sum(when is None for when, _, _ in greet)
    sometimes = sum(when.astype(jnp.int32) for when, _, _ in greet if when is not None)
    pl.semaphore_wait(barrier, always + sometimes)

    shards = [wk_ref, wv_ref, wq_ref, wo_ref]

    def slot(m, g, j, xx, cc):
        return W.at[m, g, pl.ds(pl.multiple_of(fid(j, xx, cc) * R, 32), R), :]

    def both(one, other):
        return other if one is None else one & other

    def local(m, zz, src):
        j = zz - zz // zs * zs
        return pltpu.make_async_copy(src, slot(m, h, j, x, c), l_sem.at[m, j])

    def pass_on(m, g, j, src, when=None):
        dst = slot(m, g, j, x, c)
        send(src, dst, x_send.at[m, g, j], x_recv.at[m, g, j], fid(z, 1 - x, c), h, when=when)
        send(
            src, dst, s_send.at[m, g, j, x], s_recv.at[m, g, j, x], fid(z, x, 1 - c), h, when=when
        )

    def hand_out(m, zz, src, when=None):
        home = zz // zs
        j = zz - home * zs
        used = both(when, home == h)
        guarded(used, lambda: local(m, zz, src).start())
        pass_on(m, h, j, src, when=used)
        send(
            src,
            slot(m, h, j, x, c),
            y_send.at[m, zz],
            y_recv.at[m, h, j],
            f,
            home,
            when=both(when, home != h),
        )

    def w_own(m):
        src = shards[m]
        send(src, ZL.at[m, z], z_up.at[m, z], z_recv.at[m, z], f + 4, h, when=z < Z - 1)
        send(src, ZL.at[m, z], z_dn.at[m, z], z_recv.at[m, z], f - 4, h, when=z > 0)
        hand_out(m, z, src)

    def w_along(m, d):
        below, above = z - d >= 0, z + d <= Z - 1
        for zz, ok, up in ((z - d, below, True), (z + d, above, False)):
            piece = ZL.at[m, zz]
            arrived(piece, z_recv.at[m, zz], when=ok)
            if up:
                send(piece, piece, z_up.at[m, zz], z_recv.at[m, zz], f + 4, h, when=ok & (z < Z - 1))
            else:
                send(piece, piece, z_dn.at[m, zz], z_recv.at[m, zz], f - 4, h, when=ok & (z > 0))
            hand_out(m, zz, piece, when=ok)

    def turns():
        for i in range(zs):
            yield jnp.where(z <= h * zs, i, zs - 1 - i)

    def w_heads(m):
        for j in turns():
            for step in range(1, H):
                g = head_at(step)
                piece = slot(m, g, j, x, c)
                arrived(piece, y_recv.at[m, g, j])
                pass_on(m, g, j, piece)

    def w_across(m):
        for j in turns():
            for step in range(H):
                g = head_at(step)
                piece = slot(m, g, j, 1 - x, c)
                arrived(piece, x_recv.at[m, g, j])
                send(
                    piece,
                    piece,
                    s_send.at[m, g, j, 1 - x],
                    s_recv.at[m, g, j, 1 - x],
                    fid(z, x, 1 - c),
                    h,
                )

    def w_last(m):
        for j in range(zs):
            for g in range(H):
                for xx in range(2):
                    arrived(slot(m, g, j, xx, 1 - c), s_recv.at[m, g, j, xx])
            local(m, h * zs + j, shards[m]).wait()

    w_own(0)
    table_own = pltpu.make_async_copy(
        table_ref.at[:, :, pl.ds(pl.multiple_of(h * slab, 128), slab)], table, own_sem.at[0]
    )
    table_own.start()
    queue_own = pltpu.make_async_copy(queue_ref, ZA, own_sem.at[1])
    queue_own.start()
    last = f == F - 1
    noise_own = lambda: pltpu.make_async_copy(
        noise_ref, ZB.at[pl.ds(half, half), :], own_sem.at[2]
    )
    guarded(last, lambda: noise_own().start())
    for s in range(2):

        @pl.when(f == 0)
        def _(s=s):
            KB[s, :T] = jnp.zeros((T, inner), BF16)
            VB[s, :T] = jnp.zeros((T, inner), BF16)

        @pl.when(last)
        def _(s=s):
            KB[s, 2 * T :] = jnp.zeros((T, inner), BF16)
            VB[s, 2 * T :] = jnp.zeros((T, inner), BF16)

    def tables():
        lane = lax.broadcasted_iota(jnp.int32, (1, HEAD_SIZE), 1)
        sign = jnp.where(lane < HEAD_SIZE // 2, -1.0, 1.0)
        for b in range(2):
            level = level_ref[b]
            for k in range(3):
                mod_ref[b * 3 + k : b * 3 + k + 1, :] = table[k, pl.ds(level, 1), :]
            angles = freq_ref[...] * pos_ref[b].astype(F32)
            rows = slice(b * half, (b + 1) * half)
            cos_ref[rows, :] = jnp.broadcast_to(jnp.cos(angles), (half, HEAD_SIZE))
            sin_ref[rows, :] = jnp.broadcast_to(jnp.sin(angles) * sign, (half, HEAD_SIZE))

    def sigma_step(b):
        return sigma_ref[level_ref[b] + 1] - sigma_ref[level_ref[b]]

    def modulate(s, src):
        rows = 16
        low_lanes = lax.broadcasted_iota(jnp.int32, (rows, 128), 1) < 64

        def measure(i, carry):
            at = pl.ds(pl.multiple_of(i * rows, rows), rows)
            wide = src[at, :].astype(F32)
            mean = jnp.mean(wide, axis=-1, keepdims=True)
            wide = wide - mean
            square = jnp.sum(wide * wide, axis=-1, keepdims=True)
            ST[s, h, at, :] = jnp.where(low_lanes, mean, square)
            return carry

        lax.fori_loop(0, T // rows, measure, 0)
        for step in range(1, H):
            send(ST.at[s, h], ST.at[s, h], st_send.at[s, step], st_recv.at[s, h], f, head_at(step))
        for step in range(1, H):
            g = head_at(step)
            arrived(ST.at[s, g], st_recv.at[s, g])
        for b in range(2):
            shift = mod_ref[b * 3 : b * 3 + 1, :]
            scale = 1.0 + mod_ref[b * 3 + 1 : b * 3 + 2, :]

            def body(i, carry, b=b, shift=shift, scale=scale):
                at = pl.ds(pl.multiple_of(b * half + i * rows, rows), rows)
                stats = [ST[s, g, at, :] for g in range(H)]
                means = [one[:, 0:1] for one in stats]
                mean = sum(means) / H
                square = sum(one[:, 64:65] for one in stats)
                square = square + slab * sum((one - mean) * (one - mean) for one in means)
                scale_by = lax.rsqrt(square / (H * slab) + 1e-06)
                MOD[at, :] = (
                    (src[at, :].astype(F32) - mean) * scale_by * scale + shift
                ).astype(BF16)
                return carry

            lax.fori_loop(0, half // rows, body, 0)

    depth = 1280 if slab % 1280 == 0 else slab

    def project(s, m):
        for step in list(range(1, H)) + [0]:
            g = head_at(step)

            def body(i, acc, g=g):
                at = pl.multiple_of(i * depth, 128)
                return acc + jnp.dot(
                    MOD[:, pl.ds(at, depth)],
                    W[m, g, pl.ds(at, depth), :],
                    preferred_element_type=F32,
                )

            total = lax.fori_loop(0, slab // depth, body, jnp.zeros((T, inner), F32))
            if step == 0:
                PO[m] = total
                continue
            PS[s, m, step] = total.astype(BF16)
            send(
                PS.at[s, m, step],
                PR.at[s, m, h],
                p_send.at[s, m, step],
                p_recv.at[s, m, h],
                f,
                g,
            )

    def summed(s, m):
        total = PO[m]
        for step in range(1, H):
            g = head_at(step)
            arrived(PR.at[s, m, g], p_recv.at[s, m, g])
            total = total + PR[s, m, g].astype(F32)
        return total

    def rotated(full):
        parts = []
        for i in range(heads):
            one = full[:, i * HEAD_SIZE : (i + 1) * HEAD_SIZE]
            one = one * lax.rsqrt(jnp.mean(one * one, axis=-1, keepdims=True) + 1e-06)
            turned = pltpu.roll(one, HEAD_SIZE // 2, 1)
            parts.append((one * cos_ref[...] + turned * sin_ref[...]).astype(BF16))
        return parts

    def keys(s):
        for i, part in enumerate(rotated(summed(s, 0))):
            KB[s, T : 2 * T, i * HEAD_SIZE : (i + 1) * HEAD_SIZE] = part
        halo(KB, s, k_send, k_recv)

    def values(s):
        VB[s, T : 2 * T, :] = summed(s, 1).astype(BF16)
        halo(VB, s, v_send, v_recv)

    def halo(buf, s, ssem, rsem):
        mid = buf.at[s, pl.ds(T, T), :]
        send(mid, buf.at[s, pl.ds(0, T), :], ssem.at[s, 0], rsem.at[s, 0], f + 1, h, when=f < F - 1)
        send(mid, buf.at[s, pl.ds(2 * T, T), :], ssem.at[s, 1], rsem.at[s, 1], f - 1, h, when=f > 0)

    def queries(s):
        for i, part in enumerate(rotated(summed(s, 2))):
            QB[:, i * HEAD_SIZE : (i + 1) * HEAD_SIZE] = part

    def attend(s):
        for buf, rsem in ((KB, k_recv), (VB, v_recv)):
            arrived(buf.at[s, pl.ds(0, T), :], rsem.at[s, 0], when=f > 0)
            arrived(buf.at[s, pl.ds(2 * T, T), :], rsem.at[s, 1], when=f < F - 1)
        shape = (T, 3 * T)
        qb = lax.broadcasted_iota(jnp.int32, shape, 0) // half
        kb = lax.broadcasted_iota(jnp.int32, shape, 1) // half - 2
        near = (kb - qb <= REACH) & (qb - kb <= REACH)
        near = near & (kb + 2 * f >= 0) & (kb + 2 * f < 2 * F)
        for i in range(heads):
            cols = slice(i * HEAD_SIZE, (i + 1) * HEAD_SIZE)
            scores = lax.dot_general(
                QB[:, cols], KB[s, :, cols], (((1,), (1,)), ((), ())), preferred_element_type=F32
            )
            raised = jnp.where(near, jnp.exp(scores * (1.0 / math.sqrt(HEAD_SIZE))), 0.0)
            weights = raised / jnp.sum(raised, axis=-1, keepdims=True)
            ATT[s, h, :, cols] = jnp.dot(
                weights.astype(BF16), VB[s, :, cols], preferred_element_type=F32
            ).astype(BF16)
        for step in range(1, H):
            send(ATT.at[s, h], ATT.at[s, h], t_send.at[s, step], t_recv.at[s, h], f, head_at(step))

    def attended_all(s):
        for step in range(1, H):
            g = head_at(step)
            arrived(ATT.at[s, g], t_recv.at[s, g])

    def advance(s, src):
        for n in range(chunks):
            cols = slice(n * NC, (n + 1) * NC)
            mixed = None
            for g in range(H):
                product = lax.dot_general(
                    ATT[s, g],
                    W[3, g, cols, :],
                    (((1,), (1,)), ((), ())),
                    preferred_element_type=F32,
                )
                product = product.astype(BF16).astype(F32)
                mixed = product if mixed is None else mixed + product
            for b in range(2):
                rows = slice(b * half, (b + 1) * half)
                base = src[rows, cols].astype(F32)
                gate = mod_ref[b * 3 + 2 : b * 3 + 3, cols]
                layer_out = base + gate * mixed[rows]
                following = (base + sigma_step(b) * layer_out).astype(BF16)
                if s == 1:
                    vel_ref[rows, cols] = layer_out.astype(BF16)
                    out_ref[rows, cols] = following
                elif b == 0:
                    NX[:, cols] = following
                else:
                    ZB[:half, cols] = following
            if s == 0:
                at = pl.ds(n * NC, NC)
                send(
                    NX.at[:, at],
                    ZB.at[pl.ds(half, half), at],
                    b_send.at[n],
                    b_recv.at[n],
                    f - 1,
                    h,
                    when=f > 0,
                )

    def second_state():
        for n in range(chunks):
            at = pl.ds(n * NC, NC)
            arrived(ZB.at[pl.ds(half, half), at], b_recv.at[n], when=f < F - 1)
        guarded(last, lambda: noise_own().wait())

    w_along(0, 1)
    w_own(1)
    for d in range(2, Z):
        w_along(0, d)
    w_heads(0)
    w_along(1, 1)
    queue_own.wait()
    table_own.wait()
    tables()
    modulate(0, ZA)
    w_across(0)
    w_own(2)
    for d in range(2, Z):
        w_along(1, d)
    w_heads(1)
    w_last(0)
    project(0, 0)
    w_along(2, 1)
    w_across(1)
    w_own(3)
    for d in range(2, Z):
        w_along(2, d)
    w_heads(2)
    w_last(1)
    project(0, 1)
    w_along(3, 1)
    keys(0)
    w_across(2)
    for d in range(2, Z):
        w_along(3, d)
    w_heads(3)
    w_last(2)
    project(0, 2)
    values(0)
    queries(0)
    attend(0)
    w_across(3)
    w_last(3)
    attended_all(0)
    advance(0, ZA)
    second_state()
    modulate(1, ZB)
    project(1, 0)
    project(1, 1)
    keys(1)
    project(1, 2)
    values(1)
    queries(1)
    attend(1)
    attended_all(1)
    advance(1, ZB)
    for when, action in pending:
        guarded(when, action)


def per_device(
    queue,
    noise_block,
    w_query,
    w_key,
    w_value,
    w_output,
    mod_table,
    sigma_table,
    timestep_index,
    block_position,
):
    F = lax.axis_size("frame")
    H = lax.axis_size("head")
    T, slab = queue.shape
    blocks = timestep_index.shape[0]
    half = T // blocks
    levels = mod_table.shape[0]
    R, inner = w_key.shape
    Z = F // 4
    zs = Z // H
    chunks = slab // 640
    freqs = 10000.0 ** (-np.arange(HEAD_SIZE // 2) / (HEAD_SIZE // 2))
    freqs = jnp.asarray(np.concatenate([freqs, freqs])[None, :].astype(np.float32))
    dma = pltpu.SemaphoreType.DMA
    vmem = pl.BlockSpec(memory_space=pltpu.VMEM)
    smem = pl.BlockSpec(memory_space=pltpu.SMEM)
    hbm = pl.BlockSpec(memory_space=pl.ANY)
    out = jax.ShapeDtypeStruct((T, slab), BF16)
    return pl.pallas_call(
        functools.partial(kernel, F, H),
        out_shape=(out, out),
        in_specs=[hbm] * 7 + [vmem] + [smem] * 3,
        out_specs=(vmem, vmem),
        scratch_shapes=[
            pltpu.VMEM((4, H, slab, inner), BF16),
            pltpu.VMEM((4, Z, R, inner), BF16),
            pltpu.VMEM((T, slab), BF16),
            pltpu.VMEM((T, slab), BF16),
            pltpu.VMEM((T, slab), BF16),
            pltpu.VMEM((half, slab), BF16),
            pltpu.VMEM((T, inner), BF16),
            pltpu.VMEM((2, 3 * T, inner), BF16),
            pltpu.VMEM((2, 3 * T, inner), BF16),
            pltpu.VMEM((2, H, T, inner), BF16),
            pltpu.VMEM((3, T, inner), F32),
            pltpu.VMEM((2, 3, H, T, inner), BF16),
            pltpu.VMEM((2, 3, H, T, inner), BF16),
            pltpu.VMEM((2, H, T, 128), F32),
            pltpu.VMEM((3, levels, slab), F32),
            pltpu.VMEM((blocks * 3, slab), F32),
            pltpu.VMEM((T, HEAD_SIZE), F32),
            pltpu.VMEM((T, HEAD_SIZE), F32),
            dma((3,)),
            dma((4, Z)),
            dma((4, Z)),
            dma((4, Z)),
            dma((4, Z)),
            dma((4, H, zs)),
            dma((4, H, zs)),
            dma((4, H, zs)),
            dma((4, H, zs, 2)),
            dma((4, H, zs, 2)),
            dma((4, zs)),
            dma((chunks,)),
            dma((chunks,)),
            dma((2, 2)),
            dma((2, 2)),
            dma((2, 2)),
            dma((2, 2)),
            dma((2, H)),
            dma((2, H)),
            dma((2, 3, H)),
            dma((2, 3, H)),
            dma((2, H)),
            dma((2, H)),
        ],
        compiler_params=pltpu.CompilerParams(
            collective_id=0, has_side_effects=True, vmem_limit_bytes=62 * 1024 * 1024
        ),
        cost_estimate=pl.CostEstimate(
            flops=4 * T * H * slab * inner * 4, bytes_accessed=8 * R * inner * 2, transcendentals=0
        ),
    )(
        queue,
        noise_block,
        w_key,
        w_value,
        w_query,
        w_output.T,
        jnp.transpose(mod_table, (1, 0, 2)),
        freqs,
        sigma_table,
        timestep_index,
        block_position,
    )


def solution(mesh):
    in_specs = (
        P("frame", "head"),
        P(None, "head"),
        P("frame", "head"),
        P("frame", "head"),
        P("frame", "head"),
        P("head", "frame"),
        P(),
        P(),
        P("frame"),
        P("frame"),
    )
    out_specs = (P("frame", "head"), P("frame", "head"))
    return jax.shard_map(
        per_device, mesh=mesh, in_specs=in_specs, out_specs=out_specs, check_vma=False
    )
```

time: 154 us -> 154 us (level); the launches traced: 152 us -> 154 us
  Pallas kernels: 147 us -> 149 us
    pallas_call x1, Pallas kernels: 147 us -> 149 us  [per_device(): pl.pallas_call(functools.partial(kernel, F, H), out_shape=(out, out), in_...]
where the time goes in v3:
time: 154 us
  Pallas kernels  149 us (97%)
  local copies, waits for them, and re-layouts  3.93 us (3%)
    pallas_call x1, Pallas kernels, per_device(): pl.pallas_call(functools.partial(kernel, F, H), out_shape=(out, out), in_...  149 us
    unnamed x2, local copies, waits for them, and re-layouts  3.93 us

profile of v3, /device:TPU:1, one launch (start us, length us, event | category | flops | bytes accessed | tf_op | source)
XLA Modules:
  0.0 154.0 jit_solution(7981128397289482102)
XLA Ops:
  0.6 149.5 %shard_map.122 = (bf16[128,2560]{1,0:T(8,128)(2,1)}, bf16[128,2560]{1,0:T(8,128)(2,1)}) custom-call(bf16[128,2560]{1,0:T(8,128)(2,1)} %queue_ref.1, bf16[64,2560]{1,0:T(8,128)(2,1)} %noise_ref.1, bf16[320,384]{1,0:T(8,128)(2,1)} %wk_ref.1, bf16[320,384]{1,0:T(8,128)(2,1)} %wv_ref.1, bf16[320,384]{1,0:T(8,128)(2,1)} %wq_ref.1, bf16[320,384]{1,0:T(8,128)(2,1)} %bitcast.3, ...), custom_call_target="tpu_custom_call" | custom-call | flops 4026531840 | bytes 1966080 | tf_op jit(solution)/shard_map/pallas_call | solution.py:534
  150.1 2.0 %copy.15 = bf16[128,2560]{1,0:T(8,128)(2,1)} copy(bf16[128,2560]{1,0:T(8,128)(2,1)} %get-tuple-element.4) | data formatting | bytes 1310720
  152.1 2.0 %copy.16 = bf16[128,2560]{1,0:T(8,128)(2,1)} copy(bf16[128,2560]{1,0:T(8,128)(2,1)} %get-tuple-element.5) | data formatting | bytes 1310720

commit v4 on v3

--- a/solution.py
+++ b/solution.py
@@ -61,6 +61,9 @@
     s_send,
     s_recv,
     l_sem,
+    e_up,
+    e_dn,
+    e_recv,
     b_recv,
     b_send,
     k_recv,
@@ -155,6 +158,13 @@
     def slot(m, g, j, xx, cc):
         return W.at[m, g, pl.ds(pl.multiple_of(fid(j, xx, cc) * R, 32), R), :]
 
+    along_z = (1, 3) if zs <= 2 else ()
+    in_slab = z // zs == h
+    above, below = z >= (h + 1) * zs, z < h * zs
+    rank = z - h * zs
+    extra = jnp.where(in_slab, 1 - rank, jnp.where(above, zs - 1, 0))
+    has_extra = (zs == 2) | jnp.logical_not(in_slab)
+
     def both(one, other):
         return other if one is None else one & other
 
@@ -162,9 +172,10 @@
         j = zz - zz // zs * zs
         return pltpu.make_async_copy(src, slot(m, h, j, x, c), l_sem.at[m, j])
 
-    def pass_on(m, g, j, src, when=None):
+    def pass_on(m, g, j, src, when=None, own_group=False):
         dst = slot(m, g, j, x, c)
-        send(src, dst, x_send.at[m, g, j], x_recv.at[m, g, j], fid(z, 1 - x, c), h, when=when)
+        across = both(when, j != extra) if own_group and m in along_z else when
+        send(src, dst, x_send.at[m, g, j], x_recv.at[m, g, j], fid(z, 1 - x, c), h, when=across)
         send(
             src, dst, s_send.at[m, g, j, x], s_recv.at[m, g, j, x], fid(z, x, 1 - c), h, when=when
         )
@@ -174,7 +185,7 @@
         j = zz - home * zs
         used = both(when, home == h)
         guarded(used, lambda: local(m, zz, src).start())
-        pass_on(m, h, j, src, when=used)
+        pass_on(m, h, j, src, when=used, own_group=True)
         send(
             src,
             slot(m, h, j, x, c),
@@ -192,8 +203,7 @@
         hand_out(m, z, src)
 
     def w_along(m, d):
-        below, above = z - d >= 0, z + d <= Z - 1
-        for zz, ok, up in ((z - d, below, True), (z + d, above, False)):
+        for zz, ok, up in ((z - d, z - d >= 0, True), (z + d, z + d <= Z - 1, False)):
             piece = ZL.at[m, zz]
             arrived(piece, z_recv.at[m, zz], when=ok)
             if up:
@@ -214,20 +224,47 @@
                 arrived(piece, y_recv.at[m, g, j])
                 pass_on(m, g, j, piece)
 
+    def to_sibling(m, g, j, piece, when=None):
+        send(
+            piece,
+            piece,
+            s_send.at[m, g, j, 1 - x],
+            s_recv.at[m, g, j, 1 - x],
+            fid(z, x, 1 - c),
+            h,
+            when=when,
+        )
+
+    def along(m, piece, up, down):
+        send(piece, piece, e_up.at[m], e_recv.at[m], f + 4, h, when=up & (z < Z - 1))
+        send(piece, piece, e_dn.at[m], e_recv.at[m], f - 4, h, when=down & (z > 0))
+
+    def w_swap(m):
+        piece = slot(m, h, rank, 1 - x, c)
+        arrived(piece, x_recv.at[m, h, rank], when=in_slab)
+        to_sibling(m, h, rank, piece, when=in_slab)
+        if m in along_z:
+            along(m, piece, in_slab, in_slab)
+
+    def w_extra(m):
+        if m in along_z:
+            piece = slot(m, h, extra, 1 - x, c)
+            arrived(piece, e_recv.at[m], when=has_extra)
+            to_sibling(m, h, extra, piece, when=has_extra)
+            along(m, piece, above, below)
+
     def w_across(m):
         for j in turns():
             for step in range(H):
                 g = head_at(step)
+                rest = None
+                if step == 0:
+                    rest = jnp.logical_not(in_slab & (j == rank))
+                    if m in along_z:
+                        rest = rest & (j != extra)
                 piece = slot(m, g, j, 1 - x, c)
-                arrived(piece, x_recv.at[m, g, j])
-                send(
-                    piece,
-                    piece,
-                    s_send.at[m, g, j, 1 - x],
-                    s_recv.at[m, g, j, 1 - x],
-                    fid(z, x, 1 - c),
-                    h,
-                )
+                arrived(piece, x_recv.at[m, g, j], when=rest)
+                to_sibling(m, g, j, piece, when=rest)
 
     def w_last(m):
         for j in range(zs):
@@ -236,13 +273,14 @@
                     arrived(slot(m, g, j, xx, 1 - c), s_recv.at[m, g, j, xx])
             local(m, h * zs + j, shards[m]).wait()
 
+    queue_own = pltpu.make_async_copy(queue_ref, ZA, own_sem.at[1])
+    queue_own.start()
     w_own(0)
+    w_own(1)
     table_own = pltpu.make_async_copy(
         table_ref.at[:, :, pl.ds(pl.multiple_of(h * slab, 128), slab)], table, own_sem.at[0]
     )
     table_own.start()
-    queue_own = pltpu.make_async_copy(queue_ref, ZA, own_sem.at[1])
-    queue_own.start()
     last = f == F - 1
     noise_own = lambda: pltpu.make_async_copy(
         noise_ref, ZB.at[pl.ds(half, half), :], own_sem.at[2]
@@ -275,7 +313,7 @@
     def sigma_step(b):
         return sigma_ref[level_ref[b] + 1] - sigma_ref[level_ref[b]]
 
-    def modulate(s, src):
+    def measure_rows(s, src):
         rows = 16
         low_lanes = lax.broadcasted_iota(jnp.int32, (rows, 128), 1) < 64
 
@@ -291,6 +329,9 @@
         lax.fori_loop(0, T // rows, measure, 0)
         for step in range(1, H):
             send(ST.at[s, h], ST.at[s, h], st_send.at[s, step], st_recv.at[s, h], f, head_at(step))
+
+    def modulate(s, src):
+        rows = 16
         for step in range(1, H):
             g = head_at(step)
             arrived(ST.at[s, g], st_recv.at[s, g])
@@ -447,37 +488,43 @@
             arrived(ZB.at[pl.ds(half, half), at], b_recv.at[n], when=f < F - 1)
         guarded(last, lambda: noise_own().wait())
 
+    queue_own.wait()
+    measure_rows(0, ZA)
     w_along(0, 1)
-    w_own(1)
+    w_swap(0)
     for d in range(2, Z):
         w_along(0, d)
     w_heads(0)
     w_along(1, 1)
-    queue_own.wait()
-    table_own.wait()
-    tables()
-    modulate(0, ZA)
+    w_swap(1)
     w_across(0)
     w_own(2)
     for d in range(2, Z):
         w_along(1, d)
     w_heads(1)
+    w_extra(1)
+    w_along(2, 1)
+    w_swap(2)
+    table_own.wait()
+    tables()
+    modulate(0, ZA)
     w_last(0)
     project(0, 0)
-    w_along(2, 1)
     w_across(1)
     w_own(3)
     for d in range(2, Z):
         w_along(2, d)
     w_heads(2)
+    w_along(3, 1)
+    w_swap(3)
     w_last(1)
     project(0, 1)
-    w_along(3, 1)
     keys(0)
-    w_across(2)
     for d in range(2, Z):
         w_along(3, d)
+    w_across(2)
     w_heads(3)
+    w_extra(3)
     w_last(2)
     project(0, 2)
     values(0)
@@ -488,6 +535,7 @@
     attended_all(0)
     advance(0, ZA)
     second_state()
+    measure_rows(1, ZB)
     modulate(1, ZB)
     project(1, 0)
     project(1, 1)
@@ -530,7 +578,7 @@
     vmem = pl.BlockSpec(memory_space=pltpu.VMEM)
     smem = pl.BlockSpec(memory_space=pltpu.SMEM)
     hbm = pl.BlockSpec(memory_space=pl.ANY)
-    out = jax.ShapeDtypeStruct((T, slab), BF16)
+    out = pltpu.VMEM((T, slab), BF16)
     return pl.pallas_call(
         functools.partial(kernel, F, H),
         out_shape=(out, out),
@@ -566,6 +614,9 @@
             dma((4, H, zs, 2)),
             dma((4, H, zs, 2)),
             dma((4, zs)),
+            dma((4,)),
+            dma((4,)),
+            dma((4,)),
             dma((chunks,)),
             dma((chunks,)),
             dma((2, 2)),

time: 154 us -> 147 us (0.955)
  Pallas kernels: 149 us -> 145 us
  local copies, waits for them, and re-layouts: 3.93 us -> 1.67 us
    pallas_call x1, Pallas kernels: 149 us -> 145 us  [per_device(): pl.pallas_call(functools.partial(kernel, F, H), out_shape=(out, out), in_...]
    unnamed x2, local copies, waits for them, and re-layouts: 3.93 us -> 1.67 us
where the time goes in v4:
time: 147 us
  Pallas kernels  145 us (99%)
  local copies, waits for them, and re-layouts  1.67 us (1%)
    pallas_call x1, Pallas kernels, per_device(): pl.pallas_call(functools.partial(kernel, F, H), out_shape=(out, out), in_...  145 us

profile of v4, /device:TPU:1, one launch (start us, length us, event | category | flops | bytes accessed | tf_op | source)
XLA Modules:
  0.0 147.1 jit_solution(2555021024240527732)
XLA Ops:
  0.6 144.7 %shard_map.122 = (bf16[128,2560]{1,0:T(8,128)(2,1)S(1)}, bf16[128,2560]{1,0:T(8,128)(2,1)S(1)}) custom-call(bf16[128,2560]{1,0:T(8,128)(2,1)} %queue_ref.1, bf16[64,2560]{1,0:T(8,128)(2,1)} %noise_ref.1, bf16[320,384]{1,0:T(8,128)(2,1)} %wk_ref.1, bf16[320,384]{1,0:T(8,128)(2,1)} %wv_ref.1, bf16[320,384]{1,0:T(8,128)(2,1)} %wq_ref.1, ...), custom_call_target="tpu_custom_call" | custom-call | flops 4026531840 | bytes 1966080 | tf_op jit(solution)/shard_map/pallas_call | solution.py:582
  145.4 0.8 copy.15
  146.2 0.8 copy.16

commit v5 on v4

--- a/solution.py
+++ b/solution.py
@@ -153,12 +153,16 @@
     sometimes = sum(when.astype(jnp.int32) for when, _, _ in greet if when is not None)
     pl.semaphore_wait(barrier, always + sometimes)
 
-    shards = [wk_ref, wv_ref, wq_ref, wo_ref]
+    part = R // 2
+    matrices = [wk_ref, wv_ref, wq_ref, wo_ref]
+    shards = [ref.at[pl.ds(r * part, part), :] for ref in matrices for r in range(2)]
+    M = len(shards)
 
     def slot(m, g, j, xx, cc):
-        return W.at[m, g, pl.ds(pl.multiple_of(fid(j, xx, cc) * R, 32), R), :]
-
-    along_z = (1, 3) if zs <= 2 else ()
+        at = pl.multiple_of(fid(j, xx, cc) * R + m % 2 * part, 16)
+        return W.at[m // 2, g, pl.ds(at, part), :]
+
+    along_z = range(1, M, 2) if zs <= 2 else ()
     in_slab = z // zs == h
     above, below = z >= (h + 1) * zs, z < h * zs
     rank = z - h * zs
@@ -277,6 +281,7 @@
     queue_own.start()
     w_own(0)
     w_own(1)
+    w_own(2)
     table_own = pltpu.make_async_copy(
         table_ref.at[:, :, pl.ds(pl.multiple_of(h * slab, 128), slab)], table, own_sem.at[0]
     )
@@ -490,48 +495,39 @@
 
     queue_own.wait()
     measure_rows(0, ZA)
-    w_along(0, 1)
-    w_swap(0)
-    for d in range(2, Z):
-        w_along(0, d)
-    w_heads(0)
-    w_along(1, 1)
-    w_swap(1)
-    w_across(0)
-    w_own(2)
-    for d in range(2, Z):
-        w_along(1, d)
-    w_heads(1)
-    w_extra(1)
-    w_along(2, 1)
-    w_swap(2)
-    table_own.wait()
-    tables()
-    modulate(0, ZA)
-    w_last(0)
-    project(0, 0)
-    w_across(1)
-    w_own(3)
-    for d in range(2, Z):
-        w_along(2, d)
-    w_heads(2)
-    w_along(3, 1)
-    w_swap(3)
-    w_last(1)
-    project(0, 1)
-    keys(0)
-    for d in range(2, Z):
-        w_along(3, d)
-    w_across(2)
-    w_heads(3)
-    w_extra(3)
-    w_last(2)
+    for m in range(M):
+        w_along(m, 1)
+        w_swap(m)
+        if m:
+            w_across(m - 1)
+        if m + 3 < M:
+            w_own(m + 3)
+        for d in range(2, Z):
+            w_along(m, d)
+        w_heads(m)
+        w_extra(m)
+        if m == 2:
+            table_own.wait()
+            tables()
+            modulate(0, ZA)
+        if m == 3:
+            w_last(0)
+            w_last(1)
+            project(0, 0)
+        if m == 5:
+            w_last(2)
+            w_last(3)
+            project(0, 1)
+            keys(0)
+    w_last(4)
+    w_last(5)
     project(0, 2)
     values(0)
     queries(0)
     attend(0)
-    w_across(3)
-    w_last(3)
+    w_across(M - 1)
+    w_last(6)
+    w_last(7)
     attended_all(0)
     advance(0, ZA)
     second_state()
@@ -586,7 +582,7 @@
         out_specs=(vmem, vmem),
         scratch_shapes=[
             pltpu.VMEM((4, H, slab, inner), BF16),
-            pltpu.VMEM((4, Z, R, inner), BF16),
+            pltpu.VMEM((8, Z, R // 2, inner), BF16),
             pltpu.VMEM((T, slab), BF16),
             pltpu.VMEM((T, slab), BF16),
             pltpu.VMEM((T, slab), BF16),
@@ -604,19 +600,19 @@
             pltpu.VMEM((T, HEAD_SIZE), F32),
             pltpu.VMEM((T, HEAD_SIZE), F32),
             dma((3,)),
-            dma((4, Z)),
-            dma((4, Z)),
-            dma((4, Z)),
-            dma((4, Z)),
-            dma((4, H, zs)),
-            dma((4, H, zs)),
-            dma((4, H, zs)),
-            dma((4, H, zs, 2)),
-            dma((4, H, zs, 2)),
-            dma((4, zs)),
-            dma((4,)),
-            dma((4,)),
-            dma((4,)),
+            dma((8, Z)),
+            dma((8, Z)),
+            dma((8, Z)),
+            dma((8, Z)),
+            dma((8, H, zs)),
+            dma((8, H, zs)),
+            dma((8, H, zs)),
+            dma((8, H, zs, 2)),
+            dma((8, H, zs, 2)),
+            dma((8, zs)),
+            dma((8,)),
+            dma((8,)),
+            dma((8,)),
             dma((chunks,)),
             dma((chunks,)),
             dma((2, 2)),

time: 147 us -> 144 us (0.980)
  Pallas kernels: 145 us -> 141 us
    pallas_call x1, Pallas kernels: 145 us -> 141 us  [per_device(): pl.pallas_call(functools.partial(kernel, F, H), out_shape=(out, out), in_...]
where the time goes in v5:
time: 144 us; the launch traced here: 143 us
  Pallas kernels  141 us (98%)
  local copies, waits for them, and re-layouts  1.67 us (1%)
    pallas_call x1, Pallas kernels, per_device(): pl.pallas_call(functools.partial(kernel, F, H), out_shape=(out, out), in_...  141 us

profile of v5, /device:TPU:1, one launch (start us, length us, event | category | flops | bytes accessed | tf_op | source)
XLA Modules:
  0.0 142.9 jit_solution(13690438638695019858)
XLA Ops:
  0.6 140.5 %shard_map.122 = (bf16[128,2560]{1,0:T(8,128)(2,1)S(1)}, bf16[128,2560]{1,0:T(8,128)(2,1)S(1)}) custom-call(bf16[128,2560]{1,0:T(8,128)(2,1)} %queue_ref.1, bf16[64,2560]{1,0:T(8,128)(2,1)} %noise_ref.1, bf16[320,384]{1,0:T(8,128)(2,1)} %wk_ref.1, bf16[320,384]{1,0:T(8,128)(2,1)} %wv_ref.1, bf16[320,384]{1,0:T(8,128)(2,1)} %wq_ref.1, ...), custom_call_target="tpu_custom_call" | custom-call | flops 4026531840 | bytes 1966080 | tf_op jit(solution)/shard_map/pallas_call | solution.py:578
  141.2 0.8 copy.15
  142.0 0.8 copy.16
